TPU v7x, 32 devices: a whole 2x2x4 slice. The times are simulated.
32 devices in a mesh: groups: 2 (over y), gx: 4 (over z), gy: 2 (over x), col: 2 (over core).
Axes of the slice: x: 2, y: 2, z: 4, core: 2. Of those that a mesh axis runs over, the one named last changes fastest.
Arguments:
- factors: bfloat16 [8, 16, 64, 512], P(None, None, ('groups', 'gx'), ('gy', 'col')), parts along dimension 2, may hold values from -1 to 1
- coeffs: float32 [12, 8], P('groups'), parts along dimension 0, may hold values from -3 to 3
- diffusivity: float32 [16, 64, 512], P(None, ('groups', 'gx'), ('gy', 'col')), parts along dimension 1, may hold values from 0.5 to 1.5
- terminal: float32 [16, 64, 512], P(None, ('groups', 'gx'), ('gy', 'col')), parts along dimension 1, may hold values from -6 to 6
Outputs:
- adjoint: float32 [16, 64, 512], P(None, ('groups', 'gx'), ('gy', 'col')), parts along dimension 1
- gradient: float32 [16, 64, 512], P(None, ('groups', 'gx'), ('gy', 'col')), parts along dimension 1
There are 2 independent parts, one for each index of `groups`. A program takes and returns all parts, laid end to end along the dimension named above; each array names one. Nothing has to cross between parts.
All inputs are finite; a program needn't handle non-finite values.
Results may differ from a plain program's by a relative error of at most 0.0003.
Values may be sent and summed in bfloat16 or wider, within the bound.
A program may use at most 64 MiB of HBM per device.

v0:
```python
import jax
import jax.numpy as jnp
from jax import lax
from jax.sharding import PartitionSpec as P

step_dt = 0.05


def with_halo(block, sides, width):
    for axis, dim in sides:
        count = lax.axis_size(axis)
        forward = [(i, i + 1) for i in range(count - 1)]
        backward = [(target, source) for source, target in forward]
        low = lax.ppermute(
            lax.slice_in_dim(block, block.shape[dim] - width, None, axis=dim), axis, forward
        )
        high = lax.ppermute(lax.slice_in_dim(block, 0, width, axis=dim), axis, backward)
        block = jnp.concatenate([low, block, high], axis=dim)
    return block


def neighbours(padded):
    center = padded[..., 1:-1, 1:-1]
    others = [
        padded[..., :-2, 1:-1],
        padded[..., 2:, 1:-1],
        padded[..., 1:-1, :-2],
        padded[..., 1:-1, 2:],
        jnp.roll(center, 1, -3),
        jnp.roll(center, -1, -3),
    ]
    return (center, others)


def operate(kappa_pad, field_pad):
    kappa_mid, kappa_side = neighbours(kappa_pad)
    field_mid, field_side = neighbours(field_pad)
    summed = jnp.zeros_like(field_mid)
    for kappa_near, field_near in zip(kappa_side, field_side):
        summed = summed + 0.5 * (kappa_mid + kappa_near) * (field_near - field_mid)
    return summed


def sensitivity(state_pad, field_pad):
    state_mid, state_side = neighbours(state_pad)
    field_mid, field_side = neighbours(field_pad)
    summed = jnp.zeros_like(field_mid)
    for state_near, field_near in zip(state_side, field_side):
        summed = summed + (state_near - state_mid) * (field_near - field_mid)
    return -0.5 * summed


def rebuild(factors, coeff_row):
    summed = coeff_row[0] * factors[0].astype(jnp.float32)
    for rank_index in range(1, factors.shape[0]):
        summed = summed + coeff_row[rank_index] * factors[rank_index].astype(jnp.float32)
    return summed


def per_device(factors, coeffs, diffusivity, terminal):
    steps_count = coeffs.shape[0]
    adjoint = terminal
    gradient = jnp.zeros_like(terminal)
    kappa_pad = with_halo(diffusivity, (("gx", 1), (("gy", "col"), 2)), 1)
    for step in range(steps_count - 1, -1, -1):
        state = rebuild(factors, coeffs[step])
        stacked = jnp.stack([state, adjoint])
        padded = with_halo(stacked, (("gx", 2), (("gy", "col"), 3)), 1)
        state_pad = padded[0]
        adjoint_pad = padded[1]
        gradient = gradient + step_dt * sensitivity(state_pad, adjoint_pad)
        adjoint = adjoint + step_dt * (
            operate(kappa_pad, adjoint_pad) + (1.0 - 3.0 * state * state) * adjoint
        )
    return (adjoint, gradient)


def solution(mesh):
    placed = (
        P(None, None, ("groups", "gx"), ("gy", "col")),
        P("groups", None),
        P(None, ("groups", "gx"), ("gy", "col")),
        P(None, ("groups", "gx"), ("gy", "col")),
    )
    return jax.shard_map(
        per_device,
        mesh=mesh,
        in_specs=placed,
        out_specs=(
            P(None, ("groups", "gx"), ("gy", "col")),
            P(None, ("groups", "gx"), ("gy", "col")),
        ),
        check_vma=False,
    )
```

profile of v0, /device:TPU:26, one launch (start us, length us, event | category | flops | bytes accessed | tf_op | source)
XLA Modules:
  0.0 185.6 jit_solution(12215370986752611379)
XLA Ops:
  0.6 1.7 fusion.194
  2.4 6.0 %fusion.36 = f32[1,16,8,128]{3,2,1,0:T(8,128)S(1)} fusion(f32[]{:T(128)} %bitcast.7, f32[]{:T(128)} %bitcast.6, f32[]{:T(128)} %bitcast.5, f32[]{:T(128)} %bitcast.4, f32[]{:T(128)} %bitcast.3, f32[]{:T(128)} %bitcast.2, f32[]{:T(128)} %bitcast.1, f32[]{:T(128)} %bitcast, bf16[8,16,8,128]{3,2,1,0:T(8,128)(2,1)} %param.4), kind=kLoop, calls=%fused_computation.115 | loop fusion | flops 376832 | bytes 327712 | tf_op jit(solution)/shard_map/add | solution.py:56
  8.4 2.5 %collective-permute-start.2 = (f32[2,16,1,128]{3,2,1,0:T(1,128)S(1)}, f32[2,16,1,128]{3,2,1,0:T(1,128)S(1)}, u32[]{:S(2)}, u32[]{:S(2)}) collective-permute-start(f32[2,16,1,128]{3,2,1,0:T(1,128)S(1)} %get-tuple-element.92), channel_id=1, source_target_pairs={{4,0},{8,4},{12,8},{5,1},{9,5},{13,9},{6,2},{10,6},{14,10},{7,3},{... | collective-permute-start | bytes 49160 | tf_op jit(solution)/shard_map/ppermute | solution.py:17
  13.5 5.2 %collective-permute-start.5 = (f32[16,1,128]{2,1,0:T(1,128)S(1)}, f32[16,1,128]{2,1,0:T(1,128)S(1)}, u32[]{:S(2)}, u32[]{:S(2)}) collective-permute-start(f32[16,1,128]{2,1,0:T(1,128)S(1)} %get-tuple-element.97), channel_id=1, source_target_pairs={{4,0},{8,4},{12,8},{5,1},{9,5},{13,9},{6,2},{10,6},{14,10},{7,3},{... | collective-permute-start | bytes 24584 | tf_op jit(solution)/shard_map/ppermute | solution.py:17
  20.9 5.0 %fusion.43 = f32[1,16,8,128]{3,2,1,0:T(8,128)S(1)} fusion(f32[]{:T(128)} %bitcast.18, f32[]{:T(128)} %bitcast.17, f32[]{:T(128)} %bitcast.16, f32[]{:T(128)} %bitcast.15, f32[]{:T(128)} %bitcast.14, f32[]{:T(128)} %bitcast.13, f32[]{:T(128)} %bitcast.12, f32[]{:T(128)} %bitcast.11, bf16[8,16,8,128]{3,2,1,0:T(8,128)(2,1)S(1)} %copy-done), kind=kLoop, calls=%fused_computation.122 | loop fusion | flops 376832 | bytes 327712 | tf_op jit(solution)/shard_map/add | solution.py:56
  25.9 5.1 %fusion.50 = f32[1,16,8,128]{3,2,1,0:T(8,128)S(1)} fusion(f32[]{:T(128)} %bitcast.29, f32[]{:T(128)} %bitcast.28, f32[]{:T(128)} %bitcast.27, f32[]{:T(128)} %bitcast.26, f32[]{:T(128)} %bitcast.25, f32[]{:T(128)} %bitcast.24, f32[]{:T(128)} %bitcast.23, f32[]{:T(128)} %bitcast.22, bf16[8,16,8,128]{3,2,1,0:T(8,128)(2,1)S(1)} %copy-done), kind=kLoop, calls=%fused_computation.129 | loop fusion | flops 376832 | bytes 327712 | tf_op jit(solution)/shard_map/add | solution.py:56
  31.0 4.9 %fusion.57 = f32[1,16,8,128]{3,2,1,0:T(8,128)S(1)} fusion(f32[]{:T(128)} %bitcast.40, f32[]{:T(128)} %bitcast.39, f32[]{:T(128)} %bitcast.38, f32[]{:T(128)} %bitcast.37, f32[]{:T(128)} %bitcast.36, f32[]{:T(128)} %bitcast.35, f32[]{:T(128)} %bitcast.34, f32[]{:T(128)} %bitcast.33, bf16[8,16,8,128]{3,2,1,0:T(8,128)(2,1)S(1)} %copy-done), kind=kLoop, calls=%fused_computation.136 | loop fusion | flops 376832 | bytes 327712 | tf_op jit(solution)/shard_map/add | solution.py:56
  35.9 5.2 %fusion.64 = f32[1,16,8,128]{3,2,1,0:T(8,128)S(1)} fusion(f32[]{:T(128)} %bitcast.51, f32[]{:T(128)} %bitcast.50, f32[]{:T(128)} %bitcast.49, f32[]{:T(128)} %bitcast.48, f32[]{:T(128)} %bitcast.47, f32[]{:T(128)} %bitcast.46, f32[]{:T(128)} %bitcast.45, f32[]{:T(128)} %bitcast.44, bf16[8,16,8,128]{3,2,1,0:T(8,128)(2,1)S(1)} %copy-done), kind=kLoop, calls=%fused_computation.143 | loop fusion | flops 376832 | bytes 327712 | tf_op jit(solution)/shard_map/add | solution.py:56
  41.1 5.0 %fusion.71 = f32[1,16,8,128]{3,2,1,0:T(8,128)S(1)} fusion(f32[]{:T(128)} %bitcast.62, f32[]{:T(128)} %bitcast.61, f32[]{:T(128)} %bitcast.60, f32[]{:T(128)} %bitcast.59, f32[]{:T(128)} %bitcast.58, f32[]{:T(128)} %bitcast.57, f32[]{:T(128)} %bitcast.56, f32[]{:T(128)} %bitcast.55, bf16[8,16,8,128]{3,2,1,0:T(8,128)(2,1)S(1)} %copy-done), kind=kLoop, calls=%fused_computation.150 | loop fusion | flops 376832 | bytes 327712 | tf_op jit(solution)/shard_map/add | solution.py:56
  46.3 1.9 %collective-permute-start.4 = (f32[2,16,10,1]{3,2,1,0:T(8,128)S(1)}, f32[2,16,10,1]{3,2,1,0:T(8,128)S(1)}, u32[]{:S(2)}, u32[]{:S(2)}) collective-permute-start(f32[2,16,10,1]{3,2,1,0:T(8,128)S(1)} %get-tuple-element.78), channel_id=1, source_target_pairs={{1,0},{2,1},{3,2},{5,4},{6,5},{7,6},{9,8},{10,9},{11,10},{13,12},{... | collective-permute-start | bytes 3848 | tf_op jit(solution)/shard_map/ppermute | solution.py:17
  48.3 2.4 %collective-permute-start.3 = (f32[2,16,10,1]{3,2,1,0:T(8,128)S(1)}, f32[2,16,10,1]{3,2,1,0:T(8,128)S(1)}, u32[]{:S(2)}, u32[]{:S(2)}) collective-permute-start(f32[2,16,10,1]{3,2,1,0:T(8,128)S(1)} %get-tuple-element.77), channel_id=1, source_target_pairs={{0,1},{1,2},{2,3},{4,5},{5,6},{6,7},{8,9},{9,10},{10,11},{12,13},{... | collective-permute-start | bytes 3848 | tf_op jit(solution)/shard_map/ppermute | solution.py:14
  50.8 1.9 %collective-permute-start.6 = (f32[16,10,1]{2,1,0:T(8,128)S(1)}, f32[16,10,1]{2,1,0:T(8,128)S(1)}, u32[]{:S(2)}, u32[]{:S(2)}) collective-permute-start(f32[16,10,1]{2,1,0:T(8,128)S(1)} %get-tuple-element.90), channel_id=1, source_target_pairs={{0,1},{1,2},{2,3},{4,5},{5,6},{6,7},{8,9},{9,10},{10,11},{12,13},{... | collective-permute-start | bytes 1928 | tf_op jit(solution)/shard_map/ppermute | solution.py:14
  52.7 3.6 %collective-permute-start.7 = (f32[16,10,1]{2,1,0:T(8,128)S(1)}, f32[16,10,1]{2,1,0:T(8,128)S(1)}, u32[]{:S(2)}, u32[]{:S(2)}) collective-permute-start(f32[16,10,1]{2,1,0:T(8,128)S(1)} %get-tuple-element.89), channel_id=1, source_target_pairs={{1,0},{2,1},{3,2},{5,4},{6,5},{7,6},{9,8},{10,9},{11,10},{13,12},{... | collective-permute-start | bytes 1928 | tf_op jit(solution)/shard_map/ppermute | solution.py:17
  57.4 1.5 collective-permute-done.7
  58.9 5.3 %fusion.4 = (f32[16,8,128]{2,1,0:T(8,128)S(1)}, f32[16,8,128]{2,1,0:T(8,128)S(1)}, f32[16,8,128]{2,1,0:T(8,128)S(1)}, f32[16,8,128]{2,1,0:T(8,128)S(1)}, f32[16,8,128]{2,1,0:T(8,128)S(1)}) fusion(f32[16,8,128]{2,1,0:T(8,128)S(1)} %copy-done.2, f32[16,10,130]{2,1,0:T(8,128)S(1)} %get-tuple-element.8, f32[1,8,128]{2,1,0:T(8,128)S(1)} %get-tuple-element.74, ...), kind=kLoop, calls=%fused_computation.83 | loop fusion | flops 1163264 | bytes 1328416 | tf_op jit(solution)/shard_map/add | solution.py:72
  64.2 3.9 %collective-permute-start.9 = (f32[2,16,1,128]{3,2,1,0:T(1,128)S(1)}, f32[2,16,1,128]{3,2,1,0:T(1,128)S(1)}, u32[]{:S(2)}, u32[]{:S(2)}) collective-permute-start(f32[2,16,1,128]{3,2,1,0:T(1,128)S(1)} %get-tuple-element.88), channel_id=1, source_target_pairs={{4,0},{8,4},{12,8},{5,1},{9,5},{13,9},{6,2},{10,6},{14,10},{7,3},{... | collective-permute-start | bytes 49160 | tf_op jit(solution)/shard_map/ppermute | solution.py:17
  69.5 4.2 %collective-permute-done.8 = f32[2,16,1,128]{3,2,1,0:T(1,128)S(1)} collective-permute-done((f32[2,16,1,128]{3,2,1,0:T(1,128)S(1)}, f32[2,16,1,128]{3,2,1,0:T(1,128)S(1)}, u32[]{:S(2)}, u32[]{:S(2)}) %collective-permute-start.8) | collective-permute-done | bytes 16416 | tf_op jit(solution)/shard_map/ppermute | solution.py:14
  73.9 2.4 %collective-permute-start.11 = (f32[2,16,10,1]{3,2,1,0:T(8,128)S(1)}, f32[2,16,10,1]{3,2,1,0:T(8,128)S(1)}, u32[]{:S(2)}, u32[]{:S(2)}) collective-permute-start(f32[2,16,10,1]{3,2,1,0:T(8,128)S(1)} %get-tuple-element.72), channel_id=1, source_target_pairs={{1,0},{2,1},{3,2},{5,4},{6,5},{7,6},{9,8},{10,9},{11,10},{13,12},{... | collective-permute-start | bytes 3848 | tf_op jit(solution)/shard_map/ppermute | solution.py:17
  76.3 2.0 %collective-permute-start.10 = (f32[2,16,10,1]{3,2,1,0:T(8,128)S(1)}, f32[2,16,10,1]{3,2,1,0:T(8,128)S(1)}, u32[]{:S(2)}, u32[]{:S(2)}) collective-permute-start(f32[2,16,10,1]{3,2,1,0:T(8,128)S(1)} %get-tuple-element.71), channel_id=1, source_target_pairs={{0,1},{1,2},{2,3},{4,5},{5,6},{6,7},{8,9},{9,10},{10,11},{12,13},{... | collective-permute-start | bytes 3848 | tf_op jit(solution)/shard_map/ppermute | solution.py:14
  78.4 1.8 collective-permute-done.11
  80.2 3.8 %collective-permute-done.10 = f32[2,16,10,1]{3,2,1,0:T(8,128)S(1)} collective-permute-done((f32[2,16,10,1]{3,2,1,0:T(8,128)S(1)}, f32[2,16,10,1]{3,2,1,0:T(8,128)S(1)}, u32[]{:S(2)}, u32[]{:S(2)}) %collective-permute-start.10) | collective-permute-done | bytes 1312 | tf_op jit(solution)/shard_map/ppermute | solution.py:14
  84.6 5.1 %fusion.9 = f32[16,8,128]{2,1,0:T(8,128)S(1)} fusion(f32[16,8,128]{2,1,0:T(8,128)S(1)} %get-tuple-element.2, f32[16,8,128]{2,1,0:T(8,128)S(1)} %get-tuple-element.6, f32[16,8,128]{2,1,0:T(8,128)S(1)} %get-tuple-element.5, f32[16,8,128]{2,1,0:T(8,128)S(1)} %get-tuple-element.4, f32[16,8,128]{2,1,0:T(8,128)S(1)} %get-tuple-element.3, ...), kind=kLoop, calls=%fused_computation.88 | loop fusion | flops 901120 | bytes 1196064 | tf_op jit(solution)/shard_map/add | solution.py:72
  89.8 2.4 %collective-permute-start.13 = (f32[2,16,1,128]{3,2,1,0:T(1,128)S(1)}, f32[2,16,1,128]{3,2,1,0:T(1,128)S(1)}, u32[]{:S(2)}, u32[]{:S(2)}) collective-permute-start(f32[2,16,1,128]{3,2,1,0:T(1,128)S(1)} %get-tuple-element.86), channel_id=1, source_target_pairs={{4,0},{8,4},{12,8},{5,1},{9,5},{13,9},{6,2},{10,6},{14,10},{7,3},{... | collective-permute-start | bytes 49160 | tf_op jit(solution)/shard_map/ppermute | solution.py:17
  93.6 4.2 %collective-permute-done.12 = f32[2,16,1,128]{3,2,1,0:T(1,128)S(1)} collective-permute-done((f32[2,16,1,128]{3,2,1,0:T(1,128)S(1)}, f32[2,16,1,128]{3,2,1,0:T(1,128)S(1)}, u32[]{:S(2)}, u32[]{:S(2)}) %collective-permute-start.12) | collective-permute-done | bytes 16416 | tf_op jit(solution)/shard_map/ppermute | solution.py:14
  98.0 1.9 %collective-permute-start.15 = (f32[2,16,10,1]{3,2,1,0:T(8,128)S(1)}, f32[2,16,10,1]{3,2,1,0:T(8,128)S(1)}, u32[]{:S(2)}, u32[]{:S(2)}) collective-permute-start(f32[2,16,10,1]{3,2,1,0:T(8,128)S(1)} %get-tuple-element.66), channel_id=1, source_target_pairs={{1,0},{2,1},{3,2},{5,4},{6,5},{7,6},{9,8},{10,9},{11,10},{13,12},{... | collective-permute-start | bytes 3848 | tf_op jit(solution)/shard_map/ppermute | solution.py:17
  99.9 2.4 %collective-permute-start.14 = (f32[2,16,10,1]{3,2,1,0:T(8,128)S(1)}, f32[2,16,10,1]{3,2,1,0:T(8,128)S(1)}, u32[]{:S(2)}, u32[]{:S(2)}) collective-permute-start(f32[2,16,10,1]{3,2,1,0:T(8,128)S(1)} %get-tuple-element.65), channel_id=1, source_target_pairs={{0,1},{1,2},{2,3},{4,5},{5,6},{6,7},{8,9},{9,10},{10,11},{12,13},{... | collective-permute-start | bytes 3848 | tf_op jit(solution)/shard_map/ppermute | solution.py:14
  102.4 1.4 collective-permute-done.15
  103.8 3.8 %collective-permute-done.14 = f32[2,16,10,1]{3,2,1,0:T(8,128)S(1)} collective-permute-done((f32[2,16,10,1]{3,2,1,0:T(8,128)S(1)}, f32[2,16,10,1]{3,2,1,0:T(8,128)S(1)}, u32[]{:S(2)}, u32[]{:S(2)}) %collective-permute-start.14) | collective-permute-done | bytes 1312 | tf_op jit(solution)/shard_map/ppermute | solution.py:14
  108.2 5.2 %fusion.14 = f32[16,8,128]{2,1,0:T(8,128)S(1)} fusion(f32[16,8,128]{2,1,0:T(8,128)S(1)} %fusion.9, f32[16,8,128]{2,1,0:T(8,128)S(1)} %get-tuple-element.6, f32[16,8,128]{2,1,0:T(8,128)S(1)} %get-tuple-element.5, f32[16,8,128]{2,1,0:T(8,128)S(1)} %get-tuple-element.4, f32[16,8,128]{2,1,0:T(8,128)S(1)} %get-tuple-element.3, ...), kind=kLoop, calls=%fused_computation.93 | loop fusion | flops 901120 | bytes 1196064 | tf_op jit(solution)/shard_map/add | solution.py:72
  113.5 2.2 %collective-permute-start.17 = (f32[2,16,1,128]{3,2,1,0:T(1,128)S(1)}, f32[2,16,1,128]{3,2,1,0:T(1,128)S(1)}, u32[]{:S(2)}, u32[]{:S(2)}) collective-permute-start(f32[2,16,1,128]{3,2,1,0:T(1,128)S(1)} %get-tuple-element.84), channel_id=1, source_target_pairs={{4,0},{8,4},{12,8},{5,1},{9,5},{13,9},{6,2},{10,6},{14,10},{7,3},{... | collective-permute-start | bytes 49160 | tf_op jit(solution)/shard_map/ppermute | solution.py:17
  117.1 4.2 %collective-permute-done.16 = f32[2,16,1,128]{3,2,1,0:T(1,128)S(1)} collective-permute-done((f32[2,16,1,128]{3,2,1,0:T(1,128)S(1)}, f32[2,16,1,128]{3,2,1,0:T(1,128)S(1)}, u32[]{:S(2)}, u32[]{:S(2)}) %collective-permute-start.16) | collective-permute-done | bytes 16416 | tf_op jit(solution)/shard_map/ppermute | solution.py:14
  121.5 1.9 %collective-permute-start.19 = (f32[2,16,10,1]{3,2,1,0:T(8,128)S(1)}, f32[2,16,10,1]{3,2,1,0:T(8,128)S(1)}, u32[]{:S(2)}, u32[]{:S(2)}) collective-permute-start(f32[2,16,10,1]{3,2,1,0:T(8,128)S(1)} %get-tuple-element.60), channel_id=1, source_target_pairs={{1,0},{2,1},{3,2},{5,4},{6,5},{7,6},{9,8},{10,9},{11,10},{13,12},{... | collective-permute-start | bytes 3848 | tf_op jit(solution)/shard_map/ppermute | solution.py:17
  123.4 2.4 %collective-permute-start.18 = (f32[2,16,10,1]{3,2,1,0:T(8,128)S(1)}, f32[2,16,10,1]{3,2,1,0:T(8,128)S(1)}, u32[]{:S(2)}, u32[]{:S(2)}) collective-permute-start(f32[2,16,10,1]{3,2,1,0:T(8,128)S(1)} %get-tuple-element.59), channel_id=1, source_target_pairs={{0,1},{1,2},{2,3},{4,5},{5,6},{6,7},{8,9},{9,10},{10,11},{12,13},{... | collective-permute-start | bytes 3848 | tf_op jit(solution)/shard_map/ppermute | solution.py:14
  127.3 3.8 %collective-permute-done.18 = f32[2,16,10,1]{3,2,1,0:T(8,128)S(1)} collective-permute-done((f32[2,16,10,1]{3,2,1,0:T(8,128)S(1)}, f32[2,16,10,1]{3,2,1,0:T(8,128)S(1)}, u32[]{:S(2)}, u32[]{:S(2)}) %collective-permute-start.18) | collective-permute-done | bytes 1312 | tf_op jit(solution)/shard_map/ppermute | solution.py:14
  131.8 5.1 %fusion.19 = f32[16,8,128]{2,1,0:T(8,128)S(1)} fusion(f32[16,8,128]{2,1,0:T(8,128)S(1)} %fusion.14, f32[16,8,128]{2,1,0:T(8,128)S(1)} %get-tuple-element.6, f32[16,8,128]{2,1,0:T(8,128)S(1)} %get-tuple-element.5, f32[16,8,128]{2,1,0:T(8,128)S(1)} %get-tuple-element.4, f32[16,8,128]{2,1,0:T(8,128)S(1)} %get-tuple-element.3, ...), kind=kLoop, calls=%fused_computation.98 | loop fusion | flops 901120 | bytes 1196064 | tf_op jit(solution)/shard_map/add | solution.py:72
  136.9 1.9 %collective-permute-start.21 = (f32[2,16,1,128]{3,2,1,0:T(1,128)S(1)}, f32[2,16,1,128]{3,2,1,0:T(1,128)S(1)}, u32[]{:S(2)}, u32[]{:S(2)}) collective-permute-start(f32[2,16,1,128]{3,2,1,0:T(1,128)S(1)} %get-tuple-element.82), channel_id=1, source_target_pairs={{4,0},{8,4},{12,8},{5,1},{9,5},{13,9},{6,2},{10,6},{14,10},{7,3},{... | collective-permute-start | bytes 49160 | tf_op jit(solution)/shard_map/ppermute | solution.py:17
  140.2 4.2 %collective-permute-done.20 = f32[2,16,1,128]{3,2,1,0:T(1,128)S(1)} collective-permute-done((f32[2,16,1,128]{3,2,1,0:T(1,128)S(1)}, f32[2,16,1,128]{3,2,1,0:T(1,128)S(1)}, u32[]{:S(2)}, u32[]{:S(2)}) %collective-permute-start.20) | collective-permute-done | bytes 16416 | tf_op jit(solution)/shard_map/ppermute | solution.py:14
  144.6 1.9 %collective-permute-start.23 = (f32[2,16,10,1]{3,2,1,0:T(8,128)S(1)}, f32[2,16,10,1]{3,2,1,0:T(8,128)S(1)}, u32[]{:S(2)}, u32[]{:S(2)}) collective-permute-start(f32[2,16,10,1]{3,2,1,0:T(8,128)S(1)} %get-tuple-element.54), channel_id=1, source_target_pairs={{1,0},{2,1},{3,2},{5,4},{6,5},{7,6},{9,8},{10,9},{11,10},{13,12},{... | collective-permute-start | bytes 3848 | tf_op jit(solution)/shard_map/ppermute | solution.py:17
  146.6 2.4 %collective-permute-start.22 = (f32[2,16,10,1]{3,2,1,0:T(8,128)S(1)}, f32[2,16,10,1]{3,2,1,0:T(8,128)S(1)}, u32[]{:S(2)}, u32[]{:S(2)}) collective-permute-start(f32[2,16,10,1]{3,2,1,0:T(8,128)S(1)} %get-tuple-element.53), channel_id=1, source_target_pairs={{0,1},{1,2},{2,3},{4,5},{5,6},{6,7},{8,9},{9,10},{10,11},{12,13},{... | collective-permute-start | bytes 3848 | tf_op jit(solution)/shard_map/ppermute | solution.py:14
  150.4 3.8 %collective-permute-done.22 = f32[2,16,10,1]{3,2,1,0:T(8,128)S(1)} collective-permute-done((f32[2,16,10,1]{3,2,1,0:T(8,128)S(1)}, f32[2,16,10,1]{3,2,1,0:T(8,128)S(1)}, u32[]{:S(2)}, u32[]{:S(2)}) %collective-permute-start.22) | collective-permute-done | bytes 1312 | tf_op jit(solution)/shard_map/ppermute | solution.py:14
  154.9 5.3 %fusion.24 = f32[16,8,128]{2,1,0:T(8,128)S(1)} fusion(f32[16,8,128]{2,1,0:T(8,128)S(1)} %fusion.19, f32[16,8,128]{2,1,0:T(8,128)S(1)} %get-tuple-element.6, f32[16,8,128]{2,1,0:T(8,128)S(1)} %get-tuple-element.5, f32[16,8,128]{2,1,0:T(8,128)S(1)} %get-tuple-element.4, f32[16,8,128]{2,1,0:T(8,128)S(1)} %get-tuple-element.3, ...), kind=kLoop, calls=%fused_computation.103 | loop fusion | flops 901120 | bytes 1196064 | tf_op jit(solution)/shard_map/add | solution.py:72
  160.2 1.9 %collective-permute-start.25 = (f32[2,16,1,128]{3,2,1,0:T(1,128)S(1)}, f32[2,16,1,128]{3,2,1,0:T(1,128)S(1)}, u32[]{:S(2)}, u32[]{:S(2)}) collective-permute-start(f32[2,16,1,128]{3,2,1,0:T(1,128)S(1)} %get-tuple-element.80), channel_id=1, source_target_pairs={{4,0},{8,4},{12,8},{5,1},{9,5},{13,9},{6,2},{10,6},{14,10},{7,3},{... | collective-permute-start | bytes 49160 | tf_op jit(solution)/shard_map/ppermute | solution.py:17
  163.6 4.2 %collective-permute-done.24 = f32[2,16,1,128]{3,2,1,0:T(1,128)S(1)} collective-permute-done((f32[2,16,1,128]{3,2,1,0:T(1,128)S(1)}, f32[2,16,1,128]{3,2,1,0:T(1,128)S(1)}, u32[]{:S(2)}, u32[]{:S(2)}) %collective-permute-start.24) | collective-permute-done | bytes 16416 | tf_op jit(solution)/shard_map/ppermute | solution.py:14
  167.9 1.9 %collective-permute-start.27 = (f32[2,16,10,1]{3,2,1,0:T(8,128)S(1)}, f32[2,16,10,1]{3,2,1,0:T(8,128)S(1)}, u32[]{:S(2)}, u32[]{:S(2)}) collective-permute-start(f32[2,16,10,1]{3,2,1,0:T(8,128)S(1)} %get-tuple-element.48), channel_id=1, source_target_pairs={{1,0},{2,1},{3,2},{5,4},{6,5},{7,6},{9,8},{10,9},{11,10},{13,12},{... | collective-permute-start | bytes 3848 | tf_op jit(solution)/shard_map/ppermute | solution.py:17
  169.9 2.4 %collective-permute-start.26 = (f32[2,16,10,1]{3,2,1,0:T(8,128)S(1)}, f32[2,16,10,1]{3,2,1,0:T(8,128)S(1)}, u32[]{:S(2)}, u32[]{:S(2)}) collective-permute-start(f32[2,16,10,1]{3,2,1,0:T(8,128)S(1)} %get-tuple-element.47), channel_id=1, source_target_pairs={{0,1},{1,2},{2,3},{4,5},{5,6},{6,7},{8,9},{9,10},{10,11},{12,13},{... | collective-permute-start | bytes 3848 | tf_op jit(solution)/shard_map/ppermute | solution.py:14
  173.7 3.8 %collective-permute-done.26 = f32[2,16,10,1]{3,2,1,0:T(8,128)S(1)} collective-permute-done((f32[2,16,10,1]{3,2,1,0:T(8,128)S(1)}, f32[2,16,10,1]{3,2,1,0:T(8,128)S(1)}, u32[]{:S(2)}, u32[]{:S(2)}) %collective-permute-start.26) | collective-permute-done | bytes 1312 | tf_op jit(solution)/shard_map/ppermute | solution.py:14
  178.2 1.7 fusion.77
  179.9 5.7 %fusion.29 = f32[16,8,128]{2,1,0:T(8,128)} fusion(f32[16,8,128]{2,1,0:T(8,128)S(1)} %fusion.24, f32[16,8,128]{2,1,0:T(8,128)S(1)} %get-tuple-element.6, f32[16,8,128]{2,1,0:T(8,128)S(1)} %get-tuple-element.5, f32[16,8,128]{2,1,0:T(8,128)S(1)} %get-tuple-element.4, f32[16,8,128]{2,1,0:T(8,128)S(1)} %get-tuple-element.3, ...), kind=kLoop, calls=%fused_computation.108 | loop fusion | flops 901120 | bytes 1196064 | tf_op jit(solution)/shard_map/add | solution.py:72
  (89 shorter events, 21.7 us)
Async XLA Ops:
  2.4 6.0 %copy-start.2 = (f32[16,8,128]{2,1,0:T(8,128)S(1)}, f32[16,8,128]{2,1,0:T(8,128)}, u32[]{:S(2)}) copy-start(f32[16,8,128]{2,1,0:T(8,128)} %param.7) | copy-start | bytes 196612
  2.4 9.8 %copy-start.1 = (f32[16,8,128]{2,1,0:T(8,128)S(1)}, f32[16,8,128]{2,1,0:T(8,128)}, u32[]{:S(2)}) copy-start(f32[16,8,128]{2,1,0:T(8,128)} %param.6) | copy-start | bytes 196612
  8.4 12.5 %copy-start = (bf16[8,16,8,128]{3,2,1,0:T(8,128)(2,1)S(1)}, bf16[8,16,8,128]{3,2,1,0:T(8,128)(2,1)}, u32[]{:S(2)}) copy-start(bf16[8,16,8,128]{3,2,1,0:T(8,128)(2,1)} %param.4) | copy-start | bytes 786436
  8.4 37.7 %collective-permute-start.2 = (f32[2,16,1,128]{3,2,1,0:T(1,128)S(1)}, f32[2,16,1,128]{3,2,1,0:T(1,128)S(1)}, u32[]{:S(2)}, u32[]{:S(2)}) collective-permute-start(f32[2,16,1,128]{3,2,1,0:T(1,128)S(1)} %get-tuple-element.92), channel_id=1, source_target_pairs={{4,0},{8,4},{12,8},{5,1},{9,5},{13,9},{6,2},{10,6},{14,10},{7,3},{... | collective-permute-start | bytes 49160 | tf_op jit(solution)/shard_map/ppermute | solution.py:17
  10.9 35.2 %collective-permute-start.1 = (f32[2,16,1,128]{3,2,1,0:T(1,128)S(1)}, f32[2,16,1,128]{3,2,1,0:T(1,128)S(1)}, u32[]{:S(2)}, u32[]{:S(2)}) collective-permute-start(f32[2,16,1,128]{3,2,1,0:T(1,128)S(1)} %get-tuple-element.91), channel_id=1, source_target_pairs={{0,4},{4,8},{8,12},{1,5},{5,9},{9,13},{2,6},{6,10},{10,14},{3,7},{... | collective-permute-start | bytes 49160 | tf_op jit(solution)/shard_map/ppermute | solution.py:14
  12.2 33.8 %collective-permute-start = (f32[16,1,128]{2,1,0:T(1,128)S(1)}, f32[16,1,128]{2,1,0:T(1,128)S(1)}, u32[]{:S(2)}, u32[]{:S(2)}) collective-permute-start(f32[16,1,128]{2,1,0:T(1,128)S(1)} %get-tuple-element.98), channel_id=1, source_target_pairs={{0,4},{4,8},{8,12},{1,5},{5,9},{9,13},{2,6},{6,10},{10,14},{3,7},{... | collective-permute-start | bytes 24584 | tf_op jit(solution)/shard_map/ppermute | solution.py:14
  13.5 32.6 %collective-permute-start.5 = (f32[16,1,128]{2,1,0:T(1,128)S(1)}, f32[16,1,128]{2,1,0:T(1,128)S(1)}, u32[]{:S(2)}, u32[]{:S(2)}) collective-permute-start(f32[16,1,128]{2,1,0:T(1,128)S(1)} %get-tuple-element.97), channel_id=1, source_target_pairs={{4,0},{8,4},{12,8},{5,1},{9,5},{13,9},{6,2},{10,6},{14,10},{7,3},{... | collective-permute-start | bytes 24584 | tf_op jit(solution)/shard_map/ppermute | solution.py:17
  18.7 0.7 copy-start.3
  46.3 10.0 %collective-permute-start.4 = (f32[2,16,10,1]{3,2,1,0:T(8,128)S(1)}, f32[2,16,10,1]{3,2,1,0:T(8,128)S(1)}, u32[]{:S(2)}, u32[]{:S(2)}) collective-permute-start(f32[2,16,10,1]{3,2,1,0:T(8,128)S(1)} %get-tuple-element.78), channel_id=1, source_target_pairs={{1,0},{2,1},{3,2},{5,4},{6,5},{7,6},{9,8},{10,9},{11,10},{13,12},{... | collective-permute-start | bytes 3848 | tf_op jit(solution)/shard_map/ppermute | solution.py:17
  48.3 8.1 %collective-permute-start.3 = (f32[2,16,10,1]{3,2,1,0:T(8,128)S(1)}, f32[2,16,10,1]{3,2,1,0:T(8,128)S(1)}, u32[]{:S(2)}, u32[]{:S(2)}) collective-permute-start(f32[2,16,10,1]{3,2,1,0:T(8,128)S(1)} %get-tuple-element.77), channel_id=1, source_target_pairs={{0,1},{1,2},{2,3},{4,5},{5,6},{6,7},{8,9},{9,10},{10,11},{12,13},{... | collective-permute-start | bytes 3848 | tf_op jit(solution)/shard_map/ppermute | solution.py:14
  50.8 6.6 %collective-permute-start.6 = (f32[16,10,1]{2,1,0:T(8,128)S(1)}, f32[16,10,1]{2,1,0:T(8,128)S(1)}, u32[]{:S(2)}, u32[]{:S(2)}) collective-permute-start(f32[16,10,1]{2,1,0:T(8,128)S(1)} %get-tuple-element.90), channel_id=1, source_target_pairs={{0,1},{1,2},{2,3},{4,5},{5,6},{6,7},{8,9},{9,10},{10,11},{12,13},{... | collective-permute-start | bytes 1928 | tf_op jit(solution)/shard_map/ppermute | solution.py:14
  52.7 6.1 %collective-permute-start.7 = (f32[16,10,1]{2,1,0:T(8,128)S(1)}, f32[16,10,1]{2,1,0:T(8,128)S(1)}, u32[]{:S(2)}, u32[]{:S(2)}) collective-permute-start(f32[16,10,1]{2,1,0:T(8,128)S(1)} %get-tuple-element.89), channel_id=1, source_target_pairs={{1,0},{2,1},{3,2},{5,4},{6,5},{7,6},{9,8},{10,9},{11,10},{13,12},{... | collective-permute-start | bytes 1928 | tf_op jit(solution)/shard_map/ppermute | solution.py:17
  64.2 5.4 %collective-permute-start.9 = (f32[2,16,1,128]{3,2,1,0:T(1,128)S(1)}, f32[2,16,1,128]{3,2,1,0:T(1,128)S(1)}, u32[]{:S(2)}, u32[]{:S(2)}) collective-permute-start(f32[2,16,1,128]{3,2,1,0:T(1,128)S(1)} %get-tuple-element.88), channel_id=1, source_target_pairs={{4,0},{8,4},{12,8},{5,1},{9,5},{13,9},{6,2},{10,6},{14,10},{7,3},{... | collective-permute-start | bytes 49160 | tf_op jit(solution)/shard_map/ppermute | solution.py:17
  68.1 5.6 %collective-permute-start.8 = (f32[2,16,1,128]{3,2,1,0:T(1,128)S(1)}, f32[2,16,1,128]{3,2,1,0:T(1,128)S(1)}, u32[]{:S(2)}, u32[]{:S(2)}) collective-permute-start(f32[2,16,1,128]{3,2,1,0:T(1,128)S(1)} %get-tuple-element.87), channel_id=1, source_target_pairs={{0,4},{4,8},{8,12},{1,5},{5,9},{9,13},{2,6},{6,10},{10,14},{3,7},{... | collective-permute-start | bytes 49160 | tf_op jit(solution)/shard_map/ppermute | solution.py:14
  73.9 6.2 %collective-permute-start.11 = (f32[2,16,10,1]{3,2,1,0:T(8,128)S(1)}, f32[2,16,10,1]{3,2,1,0:T(8,128)S(1)}, u32[]{:S(2)}, u32[]{:S(2)}) collective-permute-start(f32[2,16,10,1]{3,2,1,0:T(8,128)S(1)} %get-tuple-element.72), channel_id=1, source_target_pairs={{1,0},{2,1},{3,2},{5,4},{6,5},{7,6},{9,8},{10,9},{11,10},{13,12},{... | collective-permute-start | bytes 3848 | tf_op jit(solution)/shard_map/ppermute | solution.py:17
  76.3 7.7 %collective-permute-start.10 = (f32[2,16,10,1]{3,2,1,0:T(8,128)S(1)}, f32[2,16,10,1]{3,2,1,0:T(8,128)S(1)}, u32[]{:S(2)}, u32[]{:S(2)}) collective-permute-start(f32[2,16,10,1]{3,2,1,0:T(8,128)S(1)} %get-tuple-element.71), channel_id=1, source_target_pairs={{0,1},{1,2},{2,3},{4,5},{5,6},{6,7},{8,9},{9,10},{10,11},{12,13},{... | collective-permute-start | bytes 3848 | tf_op jit(solution)/shard_map/ppermute | solution.py:14
  89.8 3.8 %collective-permute-start.13 = (f32[2,16,1,128]{3,2,1,0:T(1,128)S(1)}, f32[2,16,1,128]{3,2,1,0:T(1,128)S(1)}, u32[]{:S(2)}, u32[]{:S(2)}) collective-permute-start(f32[2,16,1,128]{3,2,1,0:T(1,128)S(1)} %get-tuple-element.86), channel_id=1, source_target_pairs={{4,0},{8,4},{12,8},{5,1},{9,5},{13,9},{6,2},{10,6},{14,10},{7,3},{... | collective-permute-start | bytes 49160 | tf_op jit(solution)/shard_map/ppermute | solution.py:17
  92.1 5.6 %collective-permute-start.12 = (f32[2,16,1,128]{3,2,1,0:T(1,128)S(1)}, f32[2,16,1,128]{3,2,1,0:T(1,128)S(1)}, u32[]{:S(2)}, u32[]{:S(2)}) collective-permute-start(f32[2,16,1,128]{3,2,1,0:T(1,128)S(1)} %get-tuple-element.85), channel_id=1, source_target_pairs={{0,4},{4,8},{8,12},{1,5},{5,9},{9,13},{2,6},{6,10},{10,14},{3,7},{... | collective-permute-start | bytes 49160 | tf_op jit(solution)/shard_map/ppermute | solution.py:14
  98.0 5.8 %collective-permute-start.15 = (f32[2,16,10,1]{3,2,1,0:T(8,128)S(1)}, f32[2,16,10,1]{3,2,1,0:T(8,128)S(1)}, u32[]{:S(2)}, u32[]{:S(2)}) collective-permute-start(f32[2,16,10,1]{3,2,1,0:T(8,128)S(1)} %get-tuple-element.66), channel_id=1, source_target_pairs={{1,0},{2,1},{3,2},{5,4},{6,5},{7,6},{9,8},{10,9},{11,10},{13,12},{... | collective-permute-start | bytes 3848 | tf_op jit(solution)/shard_map/ppermute | solution.py:17
  99.9 7.7 %collective-permute-start.14 = (f32[2,16,10,1]{3,2,1,0:T(8,128)S(1)}, f32[2,16,10,1]{3,2,1,0:T(8,128)S(1)}, u32[]{:S(2)}, u32[]{:S(2)}) collective-permute-start(f32[2,16,10,1]{3,2,1,0:T(8,128)S(1)} %get-tuple-element.65), channel_id=1, source_target_pairs={{0,1},{1,2},{2,3},{4,5},{5,6},{6,7},{8,9},{9,10},{10,11},{12,13},{... | collective-permute-start | bytes 3848 | tf_op jit(solution)/shard_map/ppermute | solution.py:14
  113.5 3.6 %collective-permute-start.17 = (f32[2,16,1,128]{3,2,1,0:T(1,128)S(1)}, f32[2,16,1,128]{3,2,1,0:T(1,128)S(1)}, u32[]{:S(2)}, u32[]{:S(2)}) collective-permute-start(f32[2,16,1,128]{3,2,1,0:T(1,128)S(1)} %get-tuple-element.84), channel_id=1, source_target_pairs={{4,0},{8,4},{12,8},{5,1},{9,5},{13,9},{6,2},{10,6},{14,10},{7,3},{... | collective-permute-start | bytes 49160 | tf_op jit(solution)/shard_map/ppermute | solution.py:17
  115.7 5.6 %collective-permute-start.16 = (f32[2,16,1,128]{3,2,1,0:T(1,128)S(1)}, f32[2,16,1,128]{3,2,1,0:T(1,128)S(1)}, u32[]{:S(2)}, u32[]{:S(2)}) collective-permute-start(f32[2,16,1,128]{3,2,1,0:T(1,128)S(1)} %get-tuple-element.83), channel_id=1, source_target_pairs={{0,4},{4,8},{8,12},{1,5},{5,9},{9,13},{2,6},{6,10},{10,14},{3,7},{... | collective-permute-start | bytes 49160 | tf_op jit(solution)/shard_map/ppermute | solution.py:14
  121.5 5.8 %collective-permute-start.19 = (f32[2,16,10,1]{3,2,1,0:T(8,128)S(1)}, f32[2,16,10,1]{3,2,1,0:T(8,128)S(1)}, u32[]{:S(2)}, u32[]{:S(2)}) collective-permute-start(f32[2,16,10,1]{3,2,1,0:T(8,128)S(1)} %get-tuple-element.60), channel_id=1, source_target_pairs={{1,0},{2,1},{3,2},{5,4},{6,5},{7,6},{9,8},{10,9},{11,10},{13,12},{... | collective-permute-start | bytes 3848 | tf_op jit(solution)/shard_map/ppermute | solution.py:17
  123.4 7.7 %collective-permute-start.18 = (f32[2,16,10,1]{3,2,1,0:T(8,128)S(1)}, f32[2,16,10,1]{3,2,1,0:T(8,128)S(1)}, u32[]{:S(2)}, u32[]{:S(2)}) collective-permute-start(f32[2,16,10,1]{3,2,1,0:T(8,128)S(1)} %get-tuple-element.59), channel_id=1, source_target_pairs={{0,1},{1,2},{2,3},{4,5},{5,6},{6,7},{8,9},{9,10},{10,11},{12,13},{... | collective-permute-start | bytes 3848 | tf_op jit(solution)/shard_map/ppermute | solution.py:14
  136.9 3.4 %collective-permute-start.21 = (f32[2,16,1,128]{3,2,1,0:T(1,128)S(1)}, f32[2,16,1,128]{3,2,1,0:T(1,128)S(1)}, u32[]{:S(2)}, u32[]{:S(2)}) collective-permute-start(f32[2,16,1,128]{3,2,1,0:T(1,128)S(1)} %get-tuple-element.82), channel_id=1, source_target_pairs={{4,0},{8,4},{12,8},{5,1},{9,5},{13,9},{6,2},{10,6},{14,10},{7,3},{... | collective-permute-start | bytes 49160 | tf_op jit(solution)/shard_map/ppermute | solution.py:17
  138.8 5.6 %collective-permute-start.20 = (f32[2,16,1,128]{3,2,1,0:T(1,128)S(1)}, f32[2,16,1,128]{3,2,1,0:T(1,128)S(1)}, u32[]{:S(2)}, u32[]{:S(2)}) collective-permute-start(f32[2,16,1,128]{3,2,1,0:T(1,128)S(1)} %get-tuple-element.81), channel_id=1, source_target_pairs={{0,4},{4,8},{8,12},{1,5},{5,9},{9,13},{2,6},{6,10},{10,14},{3,7},{... | collective-permute-start | bytes 49160 | tf_op jit(solution)/shard_map/ppermute | solution.py:14
  144.6 5.8 %collective-permute-start.23 = (f32[2,16,10,1]{3,2,1,0:T(8,128)S(1)}, f32[2,16,10,1]{3,2,1,0:T(8,128)S(1)}, u32[]{:S(2)}, u32[]{:S(2)}) collective-permute-start(f32[2,16,10,1]{3,2,1,0:T(8,128)S(1)} %get-tuple-element.54), channel_id=1, source_target_pairs={{1,0},{2,1},{3,2},{5,4},{6,5},{7,6},{9,8},{10,9},{11,10},{13,12},{... | collective-permute-start | bytes 3848 | tf_op jit(solution)/shard_map/ppermute | solution.py:17
  146.6 7.7 %collective-permute-start.22 = (f32[2,16,10,1]{3,2,1,0:T(8,128)S(1)}, f32[2,16,10,1]{3,2,1,0:T(8,128)S(1)}, u32[]{:S(2)}, u32[]{:S(2)}) collective-permute-start(f32[2,16,10,1]{3,2,1,0:T(8,128)S(1)} %get-tuple-element.53), channel_id=1, source_target_pairs={{0,1},{1,2},{2,3},{4,5},{5,6},{6,7},{8,9},{9,10},{10,11},{12,13},{... | collective-permute-start | bytes 3848 | tf_op jit(solution)/shard_map/ppermute | solution.py:14
  160.2 3.4 %collective-permute-start.25 = (f32[2,16,1,128]{3,2,1,0:T(1,128)S(1)}, f32[2,16,1,128]{3,2,1,0:T(1,128)S(1)}, u32[]{:S(2)}, u32[]{:S(2)}) collective-permute-start(f32[2,16,1,128]{3,2,1,0:T(1,128)S(1)} %get-tuple-element.80), channel_id=1, source_target_pairs={{4,0},{8,4},{12,8},{5,1},{9,5},{13,9},{6,2},{10,6},{14,10},{7,3},{... | collective-permute-start | bytes 49160 | tf_op jit(solution)/shard_map/ppermute | solution.py:17
  162.1 5.6 %collective-permute-start.24 = (f32[2,16,1,128]{3,2,1,0:T(1,128)S(1)}, f32[2,16,1,128]{3,2,1,0:T(1,128)S(1)}, u32[]{:S(2)}, u32[]{:S(2)}) collective-permute-start(f32[2,16,1,128]{3,2,1,0:T(1,128)S(1)} %get-tuple-element.79), channel_id=1, source_target_pairs={{0,4},{4,8},{8,12},{1,5},{5,9},{9,13},{2,6},{6,10},{10,14},{3,7},{... | collective-permute-start | bytes 49160 | tf_op jit(solution)/shard_map/ppermute | solution.py:14
  167.9 5.8 %collective-permute-start.27 = (f32[2,16,10,1]{3,2,1,0:T(8,128)S(1)}, f32[2,16,10,1]{3,2,1,0:T(8,128)S(1)}, u32[]{:S(2)}, u32[]{:S(2)}) collective-permute-start(f32[2,16,10,1]{3,2,1,0:T(8,128)S(1)} %get-tuple-element.48), channel_id=1, source_target_pairs={{1,0},{2,1},{3,2},{5,4},{6,5},{7,6},{9,8},{10,9},{11,10},{13,12},{... | collective-permute-start | bytes 3848 | tf_op jit(solution)/shard_map/ppermute | solution.py:17
  169.9 7.7 %collective-permute-start.26 = (f32[2,16,10,1]{3,2,1,0:T(8,128)S(1)}, f32[2,16,10,1]{3,2,1,0:T(8,128)S(1)}, u32[]{:S(2)}, u32[]{:S(2)}) collective-permute-start(f32[2,16,10,1]{3,2,1,0:T(8,128)S(1)} %get-tuple-element.47), channel_id=1, source_target_pairs={{0,1},{1,2},{2,3},{4,5},{5,6},{6,7},{8,9},{9,10},{10,11},{12,13},{... | collective-permute-start | bytes 3848 | tf_op jit(solution)/shard_map/ppermute | solution.py:14
where the time goes:
time: 188 us; the launch traced here: 186 us
  other arithmetic  67.4 us (36%)
  starting transfers between devices  60.6 us (32%)
  waiting for transfers between devices  49.4 us (26%)
  local copies, waits for them, and re-layouts  6.87 us (4%)
    ppermute x14, waiting for transfers between devices, with_halo(): lax.ppermute(lax.slice_in_dim(block, block.shape[dim] - width, None, axis...  40.5 us
    ppermute x14, starting transfers between devices, with_halo(): lax.ppermute(lax.slice_in_dim(block, 0, width, axis=dim), axis, backward)  35.6 us
    add x6, other arithmetic, per_device(): adjoint + step_dt * (operate(kappa_pad, adjoint_pad) + (1.0 - 3.0 * state...  31.7 us
    add x6, other arithmetic, rebuild(): summed + coeff_row[rank_index] * factors[rank_index].astype(jnp.float32)  31.1 us
    ppermute x14, starting transfers between devices, with_halo(): lax.ppermute(lax.slice_in_dim(block, block.shape[dim] - width, None, axis...  25 us
    ppermute x14, waiting for transfers between devices, with_halo(): lax.ppermute(lax.slice_in_dim(block, 0, width, axis=dim), axis, backward)  8.89 us
  transfers between devices with their start and end apart: 28, of which 17 were waited for; matrix products, arithmetic and copies ran while one was open for 15% of the time, Pallas kernels for 0%

commit v1 on v0

v1 whole, which is shorter than its diff:
```python
import functools

import jax
import jax.numpy as jnp
from jax import lax
from jax.experimental import pallas as pl
from jax.experimental.pallas import tpu as pltpu
from jax.sharding import PartitionSpec as P

step_dt = 0.05
wide = 3

ways = ((-1, 0), (1, 0), (0, 1), (0, -1), (-1, 1), (1, -1), (-1, -1), (1, 1))
opposite = (1, 0, 3, 2, 5, 4, 7, 6)


def roll_lanes(x, shift):
    shift = shift % x.shape[-1]
    return x if shift == 0 else pltpu.roll(x, shift, x.ndim - 1)


def roll_rows(x, shift):
    return pltpu.roll(x, shift % x.shape[-2], x.ndim - 2)


def width_of(step, width):
    return max(1, width - 1 - step % width)


def stride_of(width):
    half = 1
    while half < width:
        half *= 2
    return 2 * half


def kernel(
    width, counts, factors, coeffs, kappa_in, terminal, adjoint_out, gradient_out,
    natural, row_send, row_recv, pack_send, pack_recv, send_sem, recv_sem,
):
    gx_count, gy_count, col_count = counts
    steps = coeffs.shape[0]
    ranks = factors.shape[0]
    rows = natural.shape[1] // 16
    rounds = steps // width
    group = lax.axis_index("groups")
    gx = lax.axis_index("gx")
    y = lax.axis_index("gy") * col_count + lax.axis_index("col")
    y_count = gy_count * col_count

    def inside(way):
        ok = None
        for at, move, count in ((gx, way[0], gx_count), (y, way[1], y_count)):
            if move == 0:
                continue
            here = at > 0 if move < 0 else at < count - 1
            ok = here if ok is None else jnp.logical_and(ok, here)
        return ok

    def device(way):
        far = y + way[1]
        return (group, gx + way[0], far // col_count, far % col_count)

    exists = [inside(way) for way in ways]

    barrier = pltpu.get_barrier_semaphore()
    total = jnp.int32(0)
    for m, way in enumerate(ways):
        @pl.when(exists[m])
        def _(way=way):
            pl.semaphore_signal(
                barrier, inc=1, device_id=device(way), device_id_type=pl.DeviceIdType.MESH
            )
        total = total + exists[m].astype(jnp.int32)

    for m in range(8):
        @pl.when(jnp.logical_not(exists[m]))
        def _(m=m):
            if m < 2:
                row_recv[m] = jnp.zeros(row_recv.shape[1:], jnp.float32)
            else:
                pack_recv[m - 2] = jnp.zeros(pack_recv.shape[1:], jnp.float32)

    spans = {}
    at = 0
    group_rows = []
    fields_of = [["kappa", "adjoint0"]]
    for r in range(rounds):
        fields_of.append([r * width + j for j in range(width)])
    for r in range(1, rounds):
        fields_of.append(["adjoint%d" % r])
    home = {}
    for g, names in enumerate(fields_of):
        start = at
        slot = 0
        for name in names:
            w = width_of(name, width) if isinstance(name, int) else width
            spans[name] = (at, w)
            home[name] = (g, slot)
            at += w
            slot += rows
        group_rows.append((start, at - start))

    lane = lax.broadcasted_iota(jnp.int32, (8, 128), 1)

    def copy(g, m):
        back = opposite[m]
        if m < 2:
            start, count = group_rows[g]
            source = row_send.at[m, pl.ds(start, count)]
            target = row_recv.at[back, pl.ds(start, count)]
        else:
            source = pack_send.at[g]
            target = pack_recv.at[back - 2, g]
        return pltpu.make_async_remote_copy(
            src_ref=source, dst_ref=target,
            send_sem=send_sem.at[g, m], recv_sem=recv_sem.at[g, back],
            device_id=device(ways[m]), device_id_type=pl.DeviceIdType.MESH,
        )

    def send(g, values):
        names = fields_of[g]
        stride = stride_of(spans[names[0]][1])
        slot_at = ((lane + stride // 2) % 128) // stride
        for half in range(2):
            packed = jnp.zeros((8, 128), jnp.float32)
            for name, value in zip(names, values):
                first, w = spans[name]
                row_send[0, first : first + w, half] = value[half][:w]
                row_send[1, first : first + w, half] = value[half][rows - w :]
                for x in range(rows):
                    slot = home[name][1] + x
                    moved = roll_lanes(value[half][x], slot * stride)
                    packed = jnp.where(slot_at == slot, moved, packed)
            pack_send[g, half] = packed
        for m in range(8):
            @pl.when(exists[m])
            def _(m=m):
                copy(g, m).start()

    def arrive(g):
        for m in range(8):
            @pl.when(exists[m])
            def _(m=m):
                back = opposite[m]
                if m < 2:
                    start, count = group_rows[g]
                    source = row_send.at[back, pl.ds(start, count)]
                    target = row_recv.at[m, pl.ds(start, count)]
                else:
                    source = pack_send.at[g]
                    target = pack_recv.at[m - 2, g]
                pltpu.make_async_remote_copy(
                    src_ref=source, dst_ref=target,
                    send_sem=send_sem.at[g, back], recv_sem=recv_sem.at[g, m],
                    device_id=device(ways[m]), device_id_type=pl.DeviceIdType.MESH,
                ).wait_recv()

    def padded(name, value):
        g, base = home[name]
        first, w = spans[name]
        stride = stride_of(spans[fields_of[g][0]][1])
        from_right = lane % stride < stride // 2
        center, halo = [], []
        for half in range(2):
            center.append(jnp.concatenate(
                [row_recv[0, first : first + w, half], value[half],
                 row_recv[1, first : first + w, half]], axis=0))
            own = jnp.where(from_right, pack_recv[0, g, half], pack_recv[1, g, half])
            parts = [(own, range(rows))]
            if w > 1:
                up = jnp.where(from_right, pack_recv[2, g, half], pack_recv[4, g, half])
                down = jnp.where(from_right, pack_recv[5, g, half], pack_recv[3, g, half])
                parts = [(up, range(rows - w + 1, rows)), *parts, (down, range(w - 1))]
            halo.append(jnp.stack(
                [roll_lanes(tile, -(base + x) * stride) for tile, at in parts for x in at]))
        return center, halo

    def load(ref):
        return [
            jnp.stack([ref[pl.ds(half * rows + x, 8, stride=2 * rows), :] for x in range(rows)])
            for half in range(2)
        ]

    def trim(x, extra):
        return x[extra : x.shape[0] - extra] if extra else x

    adjoint = load(terminal)
    kappa = [x * (0.5 * step_dt) for x in load(kappa_in)]
    pl.semaphore_wait(barrier, total)
    send(0, [kappa, adjoint])

    states = []
    factor = [factors[k].astype(jnp.float32) for k in range(ranks)]
    for r in range(rounds):
        for j in range(width):
            t = steps - 1 - (r * width + j)
            total_state = coeffs[t, 0] * factor[0]
            for k in range(1, ranks):
                total_state = total_state + coeffs[t, k] * factor[k]
            natural[r * width + j] = total_state.reshape(natural.shape[1:])
            states.append(load(natural.at[r * width + j]))
        send(1 + r, states[r * width : (r + 1) * width])

    last = lane == 127
    start_lane = lane == 0
    near = lane < 64
    lane_ok = jnp.logical_or(
        jnp.logical_and(near, exists[2]), jnp.logical_and(jnp.logical_not(near), exists[3]))

    def ahead(center, halo):
        c, h = roll_lanes(center, -1), roll_lanes(halo, -1)
        return jnp.where(last, h, c), jnp.where(last, c, h)

    def behind(center, halo):
        c, h = roll_lanes(center, 1), roll_lanes(halo, 1)
        return jnp.where(start_lane, h, c), jnp.where(start_lane, c, h)

    def masked(x, b):
        if b == 0:
            return x
        return jnp.concatenate(
            [jnp.where(exists[0], x[:b], 0.0), x[b : b + rows],
             jnp.where(exists[1], x[b + rows :], 0.0)], axis=0)

    arrive(0)
    kc, kh = padded("kappa", kappa)
    face_x = [[x[half][1:] + x[half][:-1] for half in range(2)] for x in (kc, kh)]
    face_y = []
    for half in range(2):
        c = trim(kc[half], 1)
        ca, ha = ahead(c, kh[half])
        face_y.append((c + ca, kh[half] + ha))
    face_z = [(x[0] + x[1], x[1] + roll_rows(x[0], -1)) for x in (kc, kh)]

    gradient = [jnp.zeros((rows, 8, 128), jnp.float32) for _ in range(2)]
    for r in range(rounds):
        if r:
            send(rounds + r, [adjoint])
            arrive(rounds + r)
        vc, vh = padded("adjoint%d" % r, adjoint)
        arrive(1 + r)
        for j in range(width):
            index = r * width + j
            a = width - j
            b = a - 1
            skip = width - a
            sc, sh = padded(index, states[index])
            sw = spans[index][1]
            new_c, new_h = [None, None], [None, None]
            for half in range(2):
                d = vc[half][1:] - vc[half][:-1]
                flux = trim(face_x[0][half], skip) * d
                new_c[half] = flux[1:] - flux[:-1]
                ds = trim(sc[half], sw - 1)
                product = (ds[1:] - ds[:-1]) * trim(d, b)
                gradient[half] = gradient[half] + (product[1:] + product[:-1])
                if b:
                    d = vh[half][1:] - vh[half][:-1]
                    flux = trim(face_x[1][half], skip) * d
                    new_h[half] = flux[1:] - flux[:-1]
            for half in range(2):
                c, h = trim(vc[half], 1), vh[half]
                ca, ha = ahead(c, h)
                dc, dh = ca - c, ha - h
                fc = trim(face_y[half][0], skip) * dc
                fh = trim(face_y[half][1], skip) * dh
                bc, bh = behind(fc, fh)
                new_c[half] = new_c[half] + (fc - bc)
                if b:
                    new_h[half] = new_h[half] + trim(fh - bh, 1)
                c, h = trim(sc[half], sw), trim(sh[half], sw - 1)
                ca, ha = ahead(c, h)
                pc = (ca - c) * trim(dc, b)
                ph = (ha - h) * trim(dh, b)
                bc, _ = behind(pc, ph)
                gradient[half] = gradient[half] + (pc + bc)
            for which, v, new, extra in ((0, vc, new_c, skip + 1), (1, vh, new_h, skip + 1)):
                if which and not b:
                    continue
                v0, v1 = trim(v[0], 1), trim(v[1], 1)
                inner, outer = v1 - v0, roll_rows(v0, -1) - v1
                fi = trim(face_z[which][0], extra) * inner
                fo = trim(face_z[which][1], extra) * outer
                new[0] = new[0] + (fi - roll_rows(fo, 1))
                new[1] = new[1] + (fo - fi)
                if not which:
                    s0, s1 = trim(sc[0], sw), trim(sc[1], sw)
                    pi = (s1 - s0) * trim(inner, b)
                    po = (roll_rows(s0, -1) - s1) * trim(outer, b)
                    gradient[0] = gradient[0] + (pi + roll_rows(po, 1))
                    gradient[1] = gradient[1] + (pi + po)
            for half in range(2):
                s = trim(sc[half], sw - b)
                v = trim(vc[half], 1)
                new_c[half] = masked(
                    v * ((1.0 + step_dt) - (3.0 * step_dt) * s * s) + new_c[half], b)
                if b:
                    s = trim(sh[half], sw - b)
                    v = trim(vh[half], 1)
                    moved = v * ((1.0 + step_dt) - (3.0 * step_dt) * s * s) + new_h[half]
                    new_h[half] = jnp.where(lane_ok, masked(moved, b - 1), 0.0)
            vc, vh = new_c, new_h
        adjoint = vc

    for half in range(2):
        for x in range(rows):
            where = pl.ds(half * rows + x, 8, stride=2 * rows)
            adjoint_out[where, :] = adjoint[half][x]
            gradient_out[where, :] = gradient[half][x] * (-0.5 * step_dt)

    for g in range(len(fields_of)):
        for m in range(8):
            @pl.when(exists[m])
            def _(g=g, m=m):
                copy(g, m).wait_send()


def per_device(counts, factors, coeffs, diffusivity, terminal):
    thick, rows, lanes = terminal.shape
    steps = coeffs.shape[0]
    width = wide
    rounds = steps // width
    groups = 2 * rounds
    sent = width * (rounds + 1) + sum(width_of(t, width) for t in range(steps))
    flat = (thick * rows, lanes)
    vmem = pl.BlockSpec(memory_space=pltpu.VMEM)
    adjoint, gradient = pl.pallas_call(
        functools.partial(kernel, width, counts),
        out_shape=[jax.ShapeDtypeStruct(flat, jnp.float32)] * 2,
        in_specs=[vmem, pl.BlockSpec(memory_space=pltpu.SMEM), vmem, vmem],
        out_specs=[vmem, vmem],
        scratch_shapes=[
            pltpu.VMEM((steps, *flat), jnp.float32),
            pltpu.VMEM((2, sent, 2, 8, lanes), jnp.float32),
            pltpu.VMEM((2, sent, 2, 8, lanes), jnp.float32),
            pltpu.VMEM((groups, 2, 8, lanes), jnp.float32),
            pltpu.VMEM((6, groups, 2, 8, lanes), jnp.float32),
            pltpu.SemaphoreType.DMA((groups, 8)),
            pltpu.SemaphoreType.DMA((groups, 8)),
        ],
        compiler_params=pltpu.CompilerParams(
            collective_id=0, has_side_effects=True, vmem_limit_bytes=32 * 1024 * 1024
        ),
    )(factors, coeffs, diffusivity.reshape(flat), terminal.reshape(flat))
    return adjoint.reshape(terminal.shape), gradient.reshape(terminal.shape)


def solution(mesh):
    block = P(None, ("groups", "gx"), ("gy", "col"))
    counts = (mesh.shape["gx"], mesh.shape["gy"], mesh.shape["col"])
    return jax.shard_map(
        functools.partial(per_device, counts),
        mesh=mesh,
        in_specs=(
            P(None, None, ("groups", "gx"), ("gy", "col")),
            P("groups", None),
            block,
            block,
        ),
        out_specs=(block, block),
        check_vma=False,
    )
```

time: 188 us -> 21.8 us (0.12)
  the two profiles are of different devices: /device:TPU:26 before, /device:TPU:1 now
where the time goes in v1:
time: 21.8 us; the launch traced here: 21.5 us
  Pallas kernels  16.3 us (75%)
  local copies, waits for them, and re-layouts  4.57 us (21%)
  between operations  0.65 us (3%)
    pallas_call x1, Pallas kernels, per_device(): pl.pallas_call(functools.partial(kernel, width, counts), out_shape=[jax.S...  16.3 us
    unnamed x10, local copies, waits for them, and re-layouts  4.57 us

profile of v1, /device:TPU:1, one launch (start us, length us, event | category | flops | bytes accessed | tf_op | source)
XLA Modules:
  0.0 21.5 jit_solution(5325949618860658147)
XLA Ops:
  0.6 0.0 copy-start
  0.6 0.9 %copy-done = bf16[8,16,8,128]{3,2,1,0:T(8,128)(2,1)S(1)} copy-done((bf16[8,16,8,128]{3,2,1,0:T(8,128)(2,1)S(1)}, bf16[8,16,8,128]{3,2,1,0:T(8,128)(2,1)}, u32[]{:S(2)}) %copy-start) | copy-done | bytes 262168
  1.6 0.0 copy-start.1
  1.6 0.8 %copy-done.1 = f32[16,8,128]{2,1,0:T(8,128)S(1)} copy-done((f32[16,8,128]{2,1,0:T(8,128)S(1)}, f32[16,8,128]{2,1,0:T(8,128)}, u32[]{:S(2)}) %copy-start.1) | copy-done | bytes 65560
  2.4 0.0 copy-start.2
  2.4 0.8 %copy-done.2 = f32[16,8,128]{2,1,0:T(8,128)S(1)} copy-done((f32[16,8,128]{2,1,0:T(8,128)S(1)}, f32[16,8,128]{2,1,0:T(8,128)}, u32[]{:S(2)}) %copy-start.2) | copy-done | bytes 65560
  3.3 0.0 copy-start.3
  3.3 0.7 %copy-done.3 = f32[6,8]{1,0:T(8,128)S(1)} copy-done((f32[6,8]{1,0:T(8,128)S(1)}, f32[6,8]{1,0:T(8,128)}, u32[]{:S(2)}) %copy-start.3) | copy-done | bytes 216
  3.9 16.3 %shard_map.59 = (f32[128,128]{1,0:T(8,128)S(1)}, f32[128,128]{1,0:T(8,128)S(1)}) custom-call(bf16[8,16,8,128]{3,2,1,0:T(8,128)(2,1)S(1)} %copy-done, f32[6,8]{1,0:T(8,128)S(1)} %copy-done.3, f32[128,128]{1,0:T(8,128)S(1)} %bitcast.4, f32[128,128]{1,0:T(8,128)S(1)} %bitcast.5), custom_call_target="tpu_custom_call" | custom-call | tf_op jit(solution)/shard_map/pallas_call | solution.py:328
  20.3 0.6 %copy.8 = f32[16,8,128]{2,1,0:T(8,128)} copy(f32[16,8,128]{2,1,0:T(8,128)S(1)} %bitcast.7) | data formatting | bytes 131072
  20.9 0.6 %copy.9 = f32[16,8,128]{2,1,0:T(8,128)} copy(f32[16,8,128]{2,1,0:T(8,128)S(1)} %bitcast.6) | data formatting | bytes 131072
Async XLA Ops:
  0.6 1.0 %copy-start = (bf16[8,16,8,128]{3,2,1,0:T(8,128)(2,1)S(1)}, bf16[8,16,8,128]{3,2,1,0:T(8,128)(2,1)}, u32[]{:S(2)}) copy-start(bf16[8,16,8,128]{3,2,1,0:T(8,128)(2,1)} %factors.1) | copy-start | bytes 786436
  1.6 0.8 %copy-start.1 = (f32[16,8,128]{2,1,0:T(8,128)S(1)}, f32[16,8,128]{2,1,0:T(8,128)}, u32[]{:S(2)}) copy-start(f32[16,8,128]{2,1,0:T(8,128)} %param.6) | copy-start | bytes 196612
  2.4 0.8 %copy-start.2 = (f32[16,8,128]{2,1,0:T(8,128)S(1)}, f32[16,8,128]{2,1,0:T(8,128)}, u32[]{:S(2)}) copy-start(f32[16,8,128]{2,1,0:T(8,128)} %param.7) | copy-start | bytes 196612
  3.3 0.7 %copy-start.3 = (f32[6,8]{1,0:T(8,128)S(1)}, f32[6,8]{1,0:T(8,128)}, u32[]{:S(2)}) copy-start(f32[6,8]{1,0:T(8,128)} %coeffs.1) | copy-start | bytes 580

commit v2 on v1

--- a/solution.py
+++ b/solution.py
@@ -8,7 +8,7 @@
 from jax.sharding import PartitionSpec as P
 
 step_dt = 0.05
-wide = 3
+wide = 6
 
 ways = ((-1, 0), (1, 0), (0, 1), (0, -1), (-1, 1), (1, -1), (-1, -1), (1, 1))
 opposite = (1, 0, 3, 2, 5, 4, 7, 6)
@@ -34,9 +34,20 @@
     return 2 * half
 
 
+def state_groups(steps, width):
+    groups = []
+    for step in range(steps):
+        key = (step // width, max(4, stride_of(width_of(step, width))))
+        if groups and groups[-1][0] == key:
+            groups[-1][1].append(step)
+        else:
+            groups.append((key, [step]))
+    return [names for _, names in groups]
+
+
 def kernel(
-    width, counts, factors, coeffs, kappa_in, terminal, adjoint_out, gradient_out,
-    natural, row_send, row_recv, pack_send, pack_recv, send_sem, recv_sem,
+    width, counts, factors_at, coeffs_at, kappa_at, terminal_at, adjoint_out, gradient_out,
+    factors, coeffs, kappa_in, terminal, load_sem, natural, row_send, row_recv, pack_send, pack_recv, send_sem, recv_sem,
 ):
     gx_count, gy_count, col_count = counts
     steps = coeffs.shape[0]
@@ -63,6 +74,15 @@
 
     exists = [inside(way) for way in ways]
 
+    loads = [
+        pltpu.make_async_copy(source, target, load_sem.at[i])
+        for i, (source, target) in enumerate(
+            ((terminal_at, terminal), (kappa_at, kappa_in), (coeffs_at, coeffs),
+             (factors_at, factors)))
+    ]
+    for copy_in in loads:
+        copy_in.start()
+
     barrier = pltpu.get_barrier_semaphore()
     total = jnp.int32(0)
     for m, way in enumerate(ways):
@@ -84,22 +104,30 @@
     spans = {}
     at = 0
     group_rows = []
-    fields_of = [["kappa", "adjoint0"]]
-    for r in range(rounds):
-        fields_of.append([r * width + j for j in range(width)])
+    by_step = state_groups(steps, width)
+    fields_of = [["kappa", "adjoint0"], *by_step]
     for r in range(1, rounds):
         fields_of.append(["adjoint%d" % r])
+    group_of = {}
     home = {}
+    tiles = 0
+    group_tiles = []
     for g, names in enumerate(fields_of):
         start = at
         slot = 0
         for name in names:
             w = width_of(name, width) if isinstance(name, int) else width
+            if name == names[0]:
+                room = 128 // stride_of(w)
             spans[name] = (at, w)
-            home[name] = (g, slot)
+            home[name] = (tiles + slot // room, slot % room)
+            group_of[name] = g
             at += w
             slot += rows
         group_rows.append((start, at - start))
+        count = -(-slot // room)
+        group_tiles.append((tiles, count))
+        tiles += count
 
     lane = lax.broadcasted_iota(jnp.int32, (8, 128), 1)
 
@@ -110,36 +138,46 @@
             source = row_send.at[m, pl.ds(start, count)]
             target = row_recv.at[back, pl.ds(start, count)]
         else:
-            source = pack_send.at[g]
-            target = pack_recv.at[back - 2, g]
+            start, count = group_tiles[g]
+            source = pack_send.at[pl.ds(start, count)]
+            target = pack_recv.at[back - 2, pl.ds(start, count)]
         return pltpu.make_async_remote_copy(
             src_ref=source, dst_ref=target,
             send_sem=send_sem.at[g, m], recv_sem=recv_sem.at[g, back],
             device_id=device(ways[m]), device_id_type=pl.DeviceIdType.MESH,
         )
 
-    def send(g, values):
+    def pack(g, values):
         names = fields_of[g]
         stride = stride_of(spans[names[0]][1])
         slot_at = ((lane + stride // 2) % 128) // stride
         for half in range(2):
-            packed = jnp.zeros((8, 128), jnp.float32)
+            packed = {}
             for name, value in zip(names, values):
                 first, w = spans[name]
                 row_send[0, first : first + w, half] = value[half][:w]
                 row_send[1, first : first + w, half] = value[half][rows - w :]
                 for x in range(rows):
-                    slot = home[name][1] + x
+                    tile, slot = home[name][0], home[name][1] + x
                     moved = roll_lanes(value[half][x], slot * stride)
-                    packed = jnp.where(slot_at == slot, moved, packed)
-            pack_send[g, half] = packed
-        for m in range(8):
+                    packed[tile] = (
+                        jnp.where(slot_at == slot, moved, packed[tile])
+                        if tile in packed else moved)
+            for tile, value in packed.items():
+                pack_send[tile, half] = value
+
+    def used(g):
+        corners = any(spans[name][1] > 1 for name in fields_of[g])
+        return range(8) if corners else range(4)
+
+    def send(g):
+        for m in used(g):
             @pl.when(exists[m])
             def _(m=m):
                 copy(g, m).start()
 
     def arrive(g):
-        for m in range(8):
+        for m in used(g):
             @pl.when(exists[m])
             def _(m=m):
                 back = opposite[m]
@@ -148,8 +186,9 @@
                     source = row_send.at[back, pl.ds(start, count)]
                     target = row_recv.at[m, pl.ds(start, count)]
                 else:
-                    source = pack_send.at[g]
-                    target = pack_recv.at[m - 2, g]
+                    start, count = group_tiles[g]
+                    source = pack_send.at[pl.ds(start, count)]
+                    target = pack_recv.at[m - 2, pl.ds(start, count)]
                 pltpu.make_async_remote_copy(
                     src_ref=source, dst_ref=target,
                     send_sem=send_sem.at[g, back], recv_sem=recv_sem.at[g, m],
@@ -157,7 +196,7 @@
                 ).wait_recv()
 
     def padded(name, value):
-        g, base = home[name]
+        g, (tile_at, base) = group_of[name], home[name]
         first, w = spans[name]
         stride = stride_of(spans[fields_of[g][0]][1])
         from_right = lane % stride < stride // 2
@@ -166,11 +205,11 @@
             center.append(jnp.concatenate(
                 [row_recv[0, first : first + w, half], value[half],
                  row_recv[1, first : first + w, half]], axis=0))
-            own = jnp.where(from_right, pack_recv[0, g, half], pack_recv[1, g, half])
+            own = jnp.where(from_right, pack_recv[0, tile_at, half], pack_recv[1, tile_at, half])
             parts = [(own, range(rows))]
             if w > 1:
-                up = jnp.where(from_right, pack_recv[2, g, half], pack_recv[4, g, half])
-                down = jnp.where(from_right, pack_recv[5, g, half], pack_recv[3, g, half])
+                up = jnp.where(from_right, pack_recv[2, tile_at, half], pack_recv[4, tile_at, half])
+                down = jnp.where(from_right, pack_recv[5, tile_at, half], pack_recv[3, tile_at, half])
                 parts = [(up, range(rows - w + 1, rows)), *parts, (down, range(w - 1))]
             halo.append(jnp.stack(
                 [roll_lanes(tile, -(base + x) * stride) for tile, at in parts for x in at]))
@@ -185,22 +224,28 @@
     def trim(x, extra):
         return x[extra : x.shape[0] - extra] if extra else x
 
+    loads[0].wait()
     adjoint = load(terminal)
+    loads[1].wait()
     kappa = [x * (0.5 * step_dt) for x in load(kappa_in)]
+    pack(0, [kappa, adjoint])
     pl.semaphore_wait(barrier, total)
-    send(0, [kappa, adjoint])
-
+    send(0)
+
+    loads[2].wait()
+    loads[3].wait()
     states = []
     factor = [factors[k].astype(jnp.float32) for k in range(ranks)]
-    for r in range(rounds):
-        for j in range(width):
-            t = steps - 1 - (r * width + j)
+    for at_group, names in enumerate(by_step):
+        for index in names:
+            t = steps - 1 - index
             total_state = coeffs[t, 0] * factor[0]
             for k in range(1, ranks):
                 total_state = total_state + coeffs[t, k] * factor[k]
-            natural[r * width + j] = total_state.reshape(natural.shape[1:])
-            states.append(load(natural.at[r * width + j]))
-        send(1 + r, states[r * width : (r + 1) * width])
+            natural[index] = total_state.reshape(natural.shape[1:])
+            states.append(load(natural.at[index]))
+        pack(1 + at_group, [states[index] for index in names])
+        send(1 + at_group)
 
     last = lane == 127
     start_lane = lane == 0
@@ -236,12 +281,14 @@
     gradient = [jnp.zeros((rows, 8, 128), jnp.float32) for _ in range(2)]
     for r in range(rounds):
         if r:
-            send(rounds + r, [adjoint])
-            arrive(rounds + r)
+            pack(len(by_step) + r, [adjoint])
+            send(len(by_step) + r)
+            arrive(len(by_step) + r)
         vc, vh = padded("adjoint%d" % r, adjoint)
-        arrive(1 + r)
         for j in range(width):
             index = r * width + j
+            if index == fields_of[group_of[index]][0]:
+                arrive(group_of[index])
             a = width - j
             b = a - 1
             skip = width - a
@@ -310,7 +357,7 @@
             gradient_out[where, :] = gradient[half][x] * (-0.5 * step_dt)
 
     for g in range(len(fields_of)):
-        for m in range(8):
+        for m in used(g):
             @pl.when(exists[m])
             def _(g=g, m=m):
                 copy(g, m).wait_send()
@@ -321,26 +368,33 @@
     steps = coeffs.shape[0]
     width = wide
     rounds = steps // width
-    groups = 2 * rounds
+    by_step = state_groups(steps, width)
+    groups = len(by_step) + rounds
+    tiles = 2 * groups
     sent = width * (rounds + 1) + sum(width_of(t, width) for t in range(steps))
     flat = (thick * rows, lanes)
     vmem = pl.BlockSpec(memory_space=pltpu.VMEM)
     adjoint, gradient = pl.pallas_call(
         functools.partial(kernel, width, counts),
         out_shape=[jax.ShapeDtypeStruct(flat, jnp.float32)] * 2,
-        in_specs=[vmem, pl.BlockSpec(memory_space=pltpu.SMEM), vmem, vmem],
+        in_specs=[pl.BlockSpec(memory_space=pltpu.HBM)] * 4,
         out_specs=[vmem, vmem],
         scratch_shapes=[
+            pltpu.VMEM(factors.shape, factors.dtype),
+            pltpu.SMEM(coeffs.shape, jnp.float32),
+            pltpu.VMEM(flat, jnp.float32),
+            pltpu.VMEM(flat, jnp.float32),
+            pltpu.SemaphoreType.DMA((4,)),
             pltpu.VMEM((steps, *flat), jnp.float32),
             pltpu.VMEM((2, sent, 2, 8, lanes), jnp.float32),
             pltpu.VMEM((2, sent, 2, 8, lanes), jnp.float32),
-            pltpu.VMEM((groups, 2, 8, lanes), jnp.float32),
-            pltpu.VMEM((6, groups, 2, 8, lanes), jnp.float32),
+            pltpu.VMEM((tiles, 2, 8, lanes), jnp.float32),
+            pltpu.VMEM((6, tiles, 2, 8, lanes), jnp.float32),
             pltpu.SemaphoreType.DMA((groups, 8)),
             pltpu.SemaphoreType.DMA((groups, 8)),
         ],
         compiler_params=pltpu.CompilerParams(
-            collective_id=0, has_side_effects=True, vmem_limit_bytes=32 * 1024 * 1024
+            collective_id=0, has_side_effects=True, vmem_limit_bytes=60 * 1024 * 1024
         ),
     )(factors, coeffs, diffusivity.reshape(flat), terminal.reshape(flat))
     return adjoint.reshape(terminal.shape), gradient.reshape(terminal.shape)

time: 21.8 us -> 18.3 us (0.84)
  the two profiles are of different devices: /device:TPU:1 before, /device:TPU:0 now
where the time goes in v2:
time: 18.3 us; the launch traced here: 18.1 us
  Pallas kernels  15.3 us (84%)
  local copies, waits for them, and re-layouts  2.14 us (12%)
  between operations  0.65 us (4%)
    pallas_call x1, Pallas kernels, per_device(): pl.pallas_call(functools.partial(kernel, width, counts), out_shape=[jax.S...  15.3 us
    unnamed x4, local copies, waits for them, and re-layouts  2.14 us

profile of v2, /device:TPU:0, one launch (start us, length us, event | category | flops | bytes accessed | tf_op | source)
XLA Modules:
  0.0 18.1 jit_solution(349444140839818071)
XLA Ops:
  0.6 15.3 %shard_map.59 = (f32[128,128]{1,0:T(8,128)}, f32[128,128]{1,0:T(8,128)}) custom-call(bf16[8,16,8,128]{3,2,1,0:T(8,128)(2,1)} %factors_at.1, f32[6,8]{1,0:T(8,128)} %coeffs_at.1, f32[128,128]{1,0:T(8,128)} %bitcast.4, f32[128,128]{1,0:T(8,128)} %bitcast.5), custom_call_target="tpu_custom_call" | custom-call | tf_op jit(solution)/shard_map/pallas_call | solution.py:377
  16.0 0.0 copy-start
  16.0 1.5 %copy.8 = f32[16,8,128]{2,1,0:T(8,128)} copy(f32[16,8,128]{2,1,0:T(8,128)} %bitcast.7) | data formatting | bytes 131072
  17.5 0.0 copy-done
  17.5 0.6 %copy.9 = f32[16,8,128]{2,1,0:T(8,128)} copy(f32[16,8,128]{2,1,0:T(8,128)S(1)} %bitcast.6) | data formatting | bytes 131072
Async XLA Ops:
  16.0 1.5 %copy-start = (f32[128,128]{1,0:T(8,128)S(1)}, f32[128,128]{1,0:T(8,128)}, u32[]{:S(2)}) copy-start(f32[128,128]{1,0:T(8,128)} %get-tuple-element.5) | copy-start | bytes 196612

commit v3 on v2

--- a/solution.py
+++ b/solution.py
@@ -32,6 +32,10 @@
     while half < width:
         half *= 2
     return 2 * half
+
+
+def near_rows(name):
+    return 2 if isinstance(name, str) and name.startswith("adjoint") else 1
 
 
 def state_groups(steps, width):
@@ -47,7 +51,8 @@
 
 def kernel(
     width, counts, factors_at, coeffs_at, kappa_at, terminal_at, adjoint_out, gradient_out,
-    factors, coeffs, kappa_in, terminal, load_sem, natural, row_send, row_recv, pack_send, pack_recv, send_sem, recv_sem,
+    factors, coeffs, kappa_in, terminal, load_sem, natural, row_send, row_recv, low_send, low_recv, pack_send, pack_recv, corner_send,
+    corner_recv, send_sem, recv_sem,
 ):
     gx_count, gy_count, col_count = counts
     steps = coeffs.shape[0]
@@ -98,12 +103,17 @@
         def _(m=m):
             if m < 2:
                 row_recv[m] = jnp.zeros(row_recv.shape[1:], jnp.float32)
+                low_recv[m] = jnp.zeros(low_recv.shape[1:], jnp.bfloat16)
+            elif m < 4:
+                pack_recv[m - 2] = jnp.zeros(pack_recv.shape[1:], jnp.float32)
             else:
-                pack_recv[m - 2] = jnp.zeros(pack_recv.shape[1:], jnp.float32)
+                corner_recv[m - 4] = jnp.zeros(corner_recv.shape[1:], jnp.bfloat16)
 
     spans = {}
-    at = 0
+    at = low_at = 0
     group_rows = []
+    low_rows = []
+    lows = {}
     by_step = state_groups(steps, width)
     fields_of = [["kappa", "adjoint0"], *by_step]
     for r in range(1, rounds):
@@ -113,7 +123,7 @@
     tiles = 0
     group_tiles = []
     for g, names in enumerate(fields_of):
-        start = at
+        row_start, low_start = at, low_at
         slot = 0
         for name in names:
             w = width_of(name, width) if isinstance(name, int) else width
@@ -122,94 +132,116 @@
             spans[name] = (at, w)
             home[name] = (tiles + slot // room, slot % room)
             group_of[name] = g
-            at += w
+            near = min(w, near_rows(name))
+            lows[name] = (low_at, near)
+            at += near
+            low_at += w - near
             slot += rows
-        group_rows.append((start, at - start))
+        group_rows.append((row_start, at - row_start))
+        low_rows.append((low_start, low_at - low_start))
         count = -(-slot // room)
         group_tiles.append((tiles, count))
         tiles += count
 
     lane = lax.broadcasted_iota(jnp.int32, (8, 128), 1)
 
-    def copy(g, m):
-        back = opposite[m]
+    def refs(g, m, to):
         if m < 2:
-            start, count = group_rows[g]
-            source = row_send.at[m, pl.ds(start, count)]
-            target = row_recv.at[back, pl.ds(start, count)]
-        else:
-            start, count = group_tiles[g]
-            source = pack_send.at[pl.ds(start, count)]
-            target = pack_recv.at[back - 2, pl.ds(start, count)]
+            span = pl.ds(*group_rows[g])
+            return row_send.at[m, span], row_recv.at[to, span]
+        if m >= 8:
+            span = pl.ds(*low_rows[g])
+            return low_send.at[m - 8, span], low_recv.at[to - 8, span]
+        span = pl.ds(*group_tiles[g])
+        if m < 4:
+            return pack_send.at[span], pack_recv.at[to - 2, span]
+        return corner_send.at[span], corner_recv.at[to - 4, span]
+
+    def turned(m):
+        return 17 - m if m >= 8 else opposite[m]
+
+    def copy(g, m, arriving=False):
+        leaves, lands = (turned(m), m) if arriving else (m, turned(m))
+        source, target = refs(g, leaves, lands)
         return pltpu.make_async_remote_copy(
             src_ref=source, dst_ref=target,
-            send_sem=send_sem.at[g, m], recv_sem=recv_sem.at[g, back],
-            device_id=device(ways[m]), device_id_type=pl.DeviceIdType.MESH,
+            send_sem=send_sem.at[g, leaves], recv_sem=recv_sem.at[g, lands],
+            device_id=device(ways[m % 8]), device_id_type=pl.DeviceIdType.MESH,
         )
 
     def pack(g, values):
         names = fields_of[g]
         stride = stride_of(spans[names[0]][1])
         slot_at = ((lane + stride // 2) % 128) // stride
-        for half in range(2):
-            packed = {}
-            for name, value in zip(names, values):
-                first, w = spans[name]
-                row_send[0, first : first + w, half] = value[half][:w]
-                row_send[1, first : first + w, half] = value[half][rows - w :]
+        packed = [{}, {}]
+        for name, value in zip(names, values):
+            (first, w), (low_first, near) = spans[name], lows[name]
+            for half in range(2):
+                row_send[0, first : first + near, half] = value[half][:near]
+                row_send[1, first : first + near, half] = value[half][rows - near :]
                 for x in range(rows):
                     tile, slot = home[name][0], home[name][1] + x
                     moved = roll_lanes(value[half][x], slot * stride)
-                    packed[tile] = (
-                        jnp.where(slot_at == slot, moved, packed[tile])
-                        if tile in packed else moved)
-            for tile, value in packed.items():
-                pack_send[tile, half] = value
+                    held = packed[half]
+                    held[tile] = (
+                        jnp.where(slot_at == slot, moved, held[tile]) if tile in held else moved)
+            if w > near:
+                both = jnp.concatenate(value, axis=1).astype(jnp.bfloat16)
+                low_send[0, low_first : low_first + w - near] = both[near:w]
+                low_send[1, low_first : low_first + w - near] = both[rows - w : rows - near]
+        for tile in packed[0]:
+            pack_send[tile, 0] = packed[0][tile]
+            pack_send[tile, 1] = packed[1][tile]
+            both = jnp.concatenate([packed[0][tile], packed[1][tile]], axis=0)
+            corner_send[tile] = both.astype(jnp.bfloat16)
 
     def used(g):
         corners = any(spans[name][1] > 1 for name in fields_of[g])
-        return range(8) if corners else range(4)
+        messages = list(range(2))
+        if low_rows[g][1]:
+            messages += [8, 9]
+        return messages + list(range(2, 8 if corners else 4))
 
     def send(g):
         for m in used(g):
-            @pl.when(exists[m])
+            @pl.when(exists[m % 8])
             def _(m=m):
                 copy(g, m).start()
 
     def arrive(g):
         for m in used(g):
-            @pl.when(exists[m])
+            @pl.when(exists[m % 8])
             def _(m=m):
-                back = opposite[m]
-                if m < 2:
-                    start, count = group_rows[g]
-                    source = row_send.at[back, pl.ds(start, count)]
-                    target = row_recv.at[m, pl.ds(start, count)]
-                else:
-                    start, count = group_tiles[g]
-                    source = pack_send.at[pl.ds(start, count)]
-                    target = pack_recv.at[m - 2, pl.ds(start, count)]
-                pltpu.make_async_remote_copy(
-                    src_ref=source, dst_ref=target,
-                    send_sem=send_sem.at[g, back], recv_sem=recv_sem.at[g, m],
-                    device_id=device(ways[m]), device_id_type=pl.DeviceIdType.MESH,
-                ).wait_recv()
+                copy(g, m, arriving=True).wait_recv()
 
     def padded(name, value):
         g, (tile_at, base) = group_of[name], home[name]
         first, w = spans[name]
         stride = stride_of(spans[fields_of[g][0]][1])
         from_right = lane % stride < stride // 2
+        low_first, near = lows[name]
         center, halo = [], []
+        outer = [[], []]
+        if w > near:
+            outer = [
+                [low_recv[side, low_first : low_first + w - near].astype(jnp.float32)]
+                for side in range(2)
+            ]
+
+        def corner(way, half):
+            return corner_recv[way - 4, tile_at].astype(jnp.float32)[8 * half : 8 * half + 8]
+
         for half in range(2):
+            part = slice(8 * half, 8 * half + 8)
             center.append(jnp.concatenate(
-                [row_recv[0, first : first + w, half], value[half],
-                 row_recv[1, first : first + w, half]], axis=0))
+                [*(x[:, part] for x in outer[0]), row_recv[0, first : first + near, half],
+                 value[half], row_recv[1, first : first + near, half],
+                 *(x[:, part] for x in outer[1])], axis=0))
             own = jnp.where(from_right, pack_recv[0, tile_at, half], pack_recv[1, tile_at, half])
             parts = [(own, range(rows))]
             if w > 1:
-                up = jnp.where(from_right, pack_recv[2, tile_at, half], pack_recv[4, tile_at, half])
-                down = jnp.where(from_right, pack_recv[5, tile_at, half], pack_recv[3, tile_at, half])
+                up = jnp.where(from_right, corner(4, half), corner(6, half))
+                down = jnp.where(from_right, corner(7, half), corner(5, half))
                 parts = [(up, range(rows - w + 1, rows)), *parts, (down, range(w - 1))]
             halo.append(jnp.stack(
                 [roll_lanes(tile, -(base + x) * stride) for tile, at in parts for x in at]))
@@ -358,7 +390,7 @@
 
     for g in range(len(fields_of)):
         for m in used(g):
-            @pl.when(exists[m])
+            @pl.when(exists[m % 8])
             def _(g=g, m=m):
                 copy(g, m).wait_send()
 
@@ -371,7 +403,10 @@
     by_step = state_groups(steps, width)
     groups = len(by_step) + rounds
     tiles = 2 * groups
-    sent = width * (rounds + 1) + sum(width_of(t, width) for t in range(steps))
+    fields = ["kappa", *("adjoint%d" % r for r in range(rounds)), *range(steps)]
+    widths = [width if isinstance(name, str) else width_of(name, width) for name in fields]
+    near = sum(min(w, near_rows(name)) for w, name in zip(widths, fields))
+    far = max(1, sum(widths) - near)
     flat = (thick * rows, lanes)
     vmem = pl.BlockSpec(memory_space=pltpu.VMEM)
     adjoint, gradient = pl.pallas_call(
@@ -386,12 +421,16 @@
             pltpu.VMEM(flat, jnp.float32),
             pltpu.SemaphoreType.DMA((4,)),
             pltpu.VMEM((steps, *flat), jnp.float32),
-            pltpu.VMEM((2, sent, 2, 8, lanes), jnp.float32),
-            pltpu.VMEM((2, sent, 2, 8, lanes), jnp.float32),
+            pltpu.VMEM((2, near, 2, 8, lanes), jnp.float32),
+            pltpu.VMEM((2, near, 2, 8, lanes), jnp.float32),
+            pltpu.VMEM((2, far, 16, lanes), jnp.bfloat16),
+            pltpu.VMEM((2, far, 16, lanes), jnp.bfloat16),
             pltpu.VMEM((tiles, 2, 8, lanes), jnp.float32),
-            pltpu.VMEM((6, tiles, 2, 8, lanes), jnp.float32),
-            pltpu.SemaphoreType.DMA((groups, 8)),
-            pltpu.SemaphoreType.DMA((groups, 8)),
+            pltpu.VMEM((2, tiles, 2, 8, lanes), jnp.float32),
+            pltpu.VMEM((tiles, 16, lanes), jnp.bfloat16),
+            pltpu.VMEM((4, tiles, 16, lanes), jnp.bfloat16),
+            pltpu.SemaphoreType.DMA((groups, 10)),
+            pltpu.SemaphoreType.DMA((groups, 10)),
         ],
         compiler_params=pltpu.CompilerParams(
             collective_id=0, has_side_effects=True, vmem_limit_bytes=60 * 1024 * 1024

time: 18.3 us -> 16.2 us (0.89)
  Pallas kernels: 15.3 us -> 13.3 us
    pallas_call x1, Pallas kernels: 15.3 us -> 13.3 us  [per_device(): pl.pallas_call(functools.partial(kernel, width, counts), out_shape=[jax.S...]
where the time goes in v3:
time: 16.2 us; the launch traced here: 16 us
  Pallas kernels  13.3 us (82%)
  local copies, waits for them, and re-layouts  2.14 us (13%)
  between operations  0.65 us (4%)
    pallas_call x1, Pallas kernels, per_device(): pl.pallas_call(functools.partial(kernel, width, counts), out_shape=[jax.S...  13.3 us
    unnamed x4, local copies, waits for them, and re-layouts  2.14 us

profile of v3, /device:TPU:0, one launch (start us, length us, event | category | flops | bytes accessed | tf_op | source)
XLA Modules:
  0.0 16.0 jit_solution(6621207299268082232)
XLA Ops:
  0.6 13.3 %shard_map.59 = (f32[128,128]{1,0:T(8,128)}, f32[128,128]{1,0:T(8,128)}) custom-call(bf16[8,16,8,128]{3,2,1,0:T(8,128)(2,1)} %factors_at.1, f32[6,8]{1,0:T(8,128)} %coeffs_at.1, f32[128,128]{1,0:T(8,128)} %bitcast.4, f32[128,128]{1,0:T(8,128)} %bitcast.5), custom_call_target="tpu_custom_call" | custom-call | tf_op jit(solution)/shard_map/pallas_call | solution.py:412
  13.9 0.0 copy-start
  13.9 1.5 %copy.8 = f32[16,8,128]{2,1,0:T(8,128)} copy(f32[16,8,128]{2,1,0:T(8,128)} %bitcast.7) | data formatting | bytes 131072
  15.4 0.0 copy-done
  15.4 0.6 %copy.9 = f32[16,8,128]{2,1,0:T(8,128)} copy(f32[16,8,128]{2,1,0:T(8,128)S(1)} %bitcast.6) | data formatting | bytes 131072
Async XLA Ops:
  13.9 1.5 %copy-start = (f32[128,128]{1,0:T(8,128)S(1)}, f32[128,128]{1,0:T(8,128)}, u32[]{:S(2)}) copy-start(f32[128,128]{1,0:T(8,128)} %get-tuple-element.5) | copy-start | bytes 196612

commit v4 on v3

--- a/solution.py
+++ b/solution.py
@@ -395,6 +395,17 @@
                 copy(g, m).wait_send()
 
 
+def store(adjoint, gradient, adjoint_out, gradient_out, sem):
+    copies = [
+        pltpu.make_async_copy(adjoint, adjoint_out, sem.at[0]),
+        pltpu.make_async_copy(gradient, gradient_out, sem.at[1]),
+    ]
+    for copy in copies:
+        copy.start()
+    for copy in copies:
+        copy.wait()
+
+
 def per_device(counts, factors, coeffs, diffusivity, terminal):
     thick, rows, lanes = terminal.shape
     steps = coeffs.shape[0]
@@ -436,6 +447,13 @@
             collective_id=0, has_side_effects=True, vmem_limit_bytes=60 * 1024 * 1024
         ),
     )(factors, coeffs, diffusivity.reshape(flat), terminal.reshape(flat))
+    adjoint, gradient = pl.pallas_call(
+        store,
+        out_shape=[jax.ShapeDtypeStruct(flat, jnp.float32)] * 2,
+        in_specs=[vmem] * 2,
+        out_specs=[pl.BlockSpec(memory_space=pltpu.HBM)] * 2,
+        scratch_shapes=[pltpu.SemaphoreType.DMA((2,))],
+    )(adjoint, gradient)
     return adjoint.reshape(terminal.shape), gradient.reshape(terminal.shape)
 
 

time: 16.2 us -> 15.6 us (0.963)
  local copies, waits for them, and re-layouts: 2.14 us -> 0 us
  Pallas kernels: 13.3 us -> 14.8 us
    unnamed x4 -> x0, local copies, waits for them, and re-layouts: 2.14 us -> none
    pallas_call x0 -> x1, Pallas kernels: none -> 1.54 us  [per_device(): pl.pallas_call(store, out_shape=[jax.ShapeDtypeStruct(flat, jnp.float32)]...]
where the time goes in v4:
time: 15.6 us; the launch traced here: 15.4 us
  Pallas kernels  14.8 us (95%)
  between operations  0.64 us (4%)
    pallas_call x1, Pallas kernels, per_device(): pl.pallas_call(functools.partial(kernel, width, counts), out_shape=[jax.S...  13.3 us
    pallas_call x1, Pallas kernels, per_device(): pl.pallas_call(store, out_shape=[jax.ShapeDtypeStruct(flat, jnp.float32)]...  1.54 us

profile of v4, /device:TPU:0, one launch (start us, length us, event | category | flops | bytes accessed | tf_op | source)
XLA Modules:
  0.0 15.4 jit_solution(3947042410956032324)
XLA Ops:
  0.6 13.3 %shard_map.59 = (f32[128,128]{1,0:T(8,128)}, f32[128,128]{1,0:T(8,128)}) custom-call(bf16[8,16,8,128]{3,2,1,0:T(8,128)(2,1)} %factors_at.1, f32[6,8]{1,0:T(8,128)} %coeffs_at.1, f32[128,128]{1,0:T(8,128)} %bitcast.4, f32[128,128]{1,0:T(8,128)} %bitcast.5), custom_call_target="tpu_custom_call" | custom-call | tf_op jit(solution)/shard_map/pallas_call | solution.py:423
  13.9 1.5 %shard_map.60 = (f32[128,128]{1,0:T(8,128)}, f32[128,128]{1,0:T(8,128)}) custom-call(f32[128,128]{1,0:T(8,128)} %get-tuple-element.6.adjoint, f32[128,128]{1,0:T(8,128)} %get-tuple-element.7.gradient), custom_call_target="tpu_custom_call" | custom-call | tf_op jit(solution)/shard_map/pallas_call | solution.py:450

commit v5 on v4

--- a/solution.py
+++ b/solution.py
@@ -200,7 +200,7 @@
         messages = list(range(2))
         if low_rows[g][1]:
             messages += [8, 9]
-        return messages + list(range(2, 8 if corners else 4))
+        return list(range(4, 8 if corners else 4)) + messages + [2, 3]
 
     def send(g):
         for m in used(g):

time: 15.6 us -> 15.1 us (0.968)
  Pallas kernels: 14.8 us -> 14.2 us
    pallas_call x1, Pallas kernels: 13.3 us -> 12.7 us  [per_device(): pl.pallas_call(functools.partial(kernel, width, counts), out_shape=[jax.S...]
where the time goes in v5:
time: 15.1 us; the launch traced here: 14.8 us
  Pallas kernels  14.2 us (94%)
  between operations  0.64 us (4%)
    pallas_call x1, Pallas kernels, per_device(): pl.pallas_call(functools.partial(kernel, width, counts), out_shape=[jax.S...  12.7 us
    pallas_call x1, Pallas kernels, per_device(): pl.pallas_call(store, out_shape=[jax.ShapeDtypeStruct(flat, jnp.float32)]...  1.54 us

profile of v5, /device:TPU:0, one launch (start us, length us, event | category | flops | bytes accessed | tf_op | source)
XLA Modules:
  0.0 14.8 jit_solution(5321355681639278757)
XLA Ops:
  0.6 12.7 %shard_map.59 = (f32[128,128]{1,0:T(8,128)}, f32[128,128]{1,0:T(8,128)}) custom-call(bf16[8,16,8,128]{3,2,1,0:T(8,128)(2,1)} %factors_at.1, f32[6,8]{1,0:T(8,128)} %coeffs_at.1, f32[128,128]{1,0:T(8,128)} %bitcast.4, f32[128,128]{1,0:T(8,128)} %bitcast.5), custom_call_target="tpu_custom_call" | custom-call | tf_op jit(solution)/shard_map/pallas_call | solution.py:423
  13.3 1.5 %shard_map.60 = (f32[128,128]{1,0:T(8,128)}, f32[128,128]{1,0:T(8,128)}) custom-call(f32[128,128]{1,0:T(8,128)} %get-tuple-element.6.adjoint, f32[128,128]{1,0:T(8,128)} %get-tuple-element.7.gradient), custom_call_target="tpu_custom_call" | custom-call | tf_op jit(solution)/shard_map/pallas_call | solution.py:450
